TPU v7x, 32 devices: a whole 2x2x4 slice. The times are simulated.
32 devices in a mesh: parts: 2 (over x), feat: 8 (over z, y), tok: 2 (over core).
Axes of the slice: x: 2, y: 2, z: 4, core: 2. Of those that a mesh axis runs over, the one named last changes fastest.
Arguments:
- token_index: int32 [16, 16], P(('parts', 'feat')), parts along dimension 0, may hold values from 0 to 15, each once within a row
- act_pool: bfloat16 [256, 14336], P(('parts', 'feat'), 'tok'), parts along dimension 0, may hold values from -6 to 6
- grad_pool: bfloat16 [256, 4096], P(('parts', 'feat'), 'tok'), parts along dimension 0, may hold values from -6 to 6
- basis_in: bfloat16 [28672, 14336], P(('parts', 'tok'), 'feat'), parts along dimension 0, may hold values from -0.046875 to 0.046875
- basis_out: bfloat16 [8192, 4096], P(('parts', 'tok'), 'feat'), parts along dimension 0, may hold values from -0.09375 to 0.09375
- precond: bfloat16 [4, 4096, 14336], P('parts', None, ('feat', 'tok')), parts along dimension 0, may hold values from -0.0007324219 to 0.0007324219
Outputs:
- scores: float32 [4, 128], P('parts'), parts along dimension 0
- act_rot: bfloat16 [256, 14336], P('parts', ('feat', 'tok')), parts along dimension 0
- grad_rot: bfloat16 [256, 4096], P('parts', ('feat', 'tok')), parts along dimension 0
There are 2 independent parts, one for each index of `parts`. A program takes and returns all parts, laid end to end along the dimension named above; each array names one. Nothing has to cross between parts.
Inputs may be any that keep to these rules, and one draw needn't show every extreme that they name: Each row of token_index orders the 16 stored tokens of one shard, each once.
All inputs are finite; a program needn't handle non-finite values.
Results may differ from a plain program's by a relative error of at most 0.006.
Values may be sent and summed in bfloat16 or wider, within the bound.
No kernel may reach another device: no remote copies, remote signals or barrier semaphores. Data moves between devices by JAX's collectives and lax.ppermute only.
A program may use at most 128 MiB of HBM per device.

v0:
```python
import jax
import jax.numpy as jnp
from jax import lax
from jax.sharding import PartitionSpec as P


def shards(token_index, act_pool, grad_pool, basis_in, basis_out, precond):
    order = token_index[0]
    act = jnp.take(act_pool, order, axis=0)
    grads = jnp.take(grad_pool, order, axis=0)
    act_part = jnp.dot(
        lax.all_gather(act, "feat", axis=0, tiled=True),
        basis_in,
        preferred_element_type=jnp.float32,
    )
    act_rot = lax.psum_scatter(act_part, "tok", scatter_dimension=1, tiled=True).astype(
        jnp.bfloat16
    )
    grad_part = jnp.dot(
        lax.all_gather(grads, "feat", axis=0, tiled=True),
        basis_out,
        preferred_element_type=jnp.float32,
    )
    grad_block = lax.psum(grad_part, "tok").astype(jnp.bfloat16)
    width = grad_block.shape[1] // lax.axis_size("tok")
    grad_rot = lax.dynamic_slice_in_dim(grad_block, lax.axis_index("tok") * width, width, 1)
    inner = jnp.einsum("tj,qkj->qtk", act_rot, precond, preferred_element_type=jnp.float32)
    partial_value = jnp.einsum(
        "tk,qtk->qt",
        lax.all_gather(grad_block, "feat", axis=1, tiled=True).astype(jnp.float32),
        inner,
    )
    scores = lax.psum(partial_value, ("feat", "tok"))
    return (scores, act_rot, grad_rot)


def solution(mesh):
    placed = (
        P(("parts", "feat"), None),
        P(("parts", "feat"), "tok"),
        P(("parts", "feat"), "tok"),
        P(("parts", "tok"), "feat"),
        P(("parts", "tok"), "feat"),
        P("parts", None, ("feat", "tok")),
    )
    return jax.shard_map(
        shards,
        mesh=mesh,
        in_specs=placed,
        out_specs=(P("parts", None), P("parts", ("feat", "tok")), P("parts", ("feat", "tok"))),
        check_vma=False,
    )
```

profile of v0, /device:TPU:0, one launch (start us, length us, event | category | flops | bytes accessed | tf_op | source)
XLA Modules:
  0.0 193.2 jit_solution(4575321465842306864)
XLA Ops:
  7.2 0.0 copy-start
  7.2 0.0 all-gather.3.cloned.1.call-start
  7.2 0.8 compare_and_fusion
  8.0 0.7 fusion.4
  8.7 1.9 gather_fusion
  10.6 0.8 broadcast_select_fusion
  11.3 0.0 all-gather.3.cloned.1.call-update
  11.4 0.0 copy-start.1
  11.4 0.0 reduce-scatter.2.cloned.1.call-start
  11.4 49.0 %all-gather.3.cloned.1.call-done = bf16[128,7168]{1,0:T(8,128)(2,1)} async-done(((bf16[16,7168]{1,0:T(8,128)(2,1)}), bf16[128,7168]{1,0:T(8,128)(2,1)}) %all-gather.3.cloned.1.call-update) | async-done | bytes 1835024 | tf_op jit(solution)/shard_map/all_gather | solution.py:12
  60.5 13.3 %fusion.5 = f32[128,1792]{1,0:T(8,128)} fusion(bf16[128,7168]{1,0:T(8,128)(2,1)} %all-gather.3.cloned.1.call-done, bf16[7168,1792]{1,0:T(8,128)(2,1)} %param.9), kind=kOutput, calls=%fused_computation.15 | convolution fusion | flops 3288334336 | bytes 28442624 | tf_op jit(solution)/shard_map/dot_general | solution.py:11
  73.8 0.0 reduce-scatter.2.cloned.1.call-update
  73.8 0.0 all-gather.5.cloned.1.call-start
  73.8 0.0 copy-done.1
  73.8 0.6 gather_fusion.1
  74.4 0.1 broadcast_select_fusion.1
  74.5 31.3 %all_gather.10 = bf16[128,2048]{1,0:T(8,128)(2,1)S(1)} all-gather(bf16[16,2048]{1,0:T(8,128)(2,1)S(1)} %broadcast_select_fusion.1), channel_id=1, replica_groups=mesh['parts'=2,'feat'=8,'tok'=2] {'feat'}, dimensions={0}, use_global_device_ids=true | all-gather | bytes 589824 | tf_op jit(solution)/shard_map/all_gather | solution.py:20
  105.8 0.0 copy-done
  105.8 0.4 fusion.6
  106.2 4.7 %all-reduce.1 = bf16[128,512]{1,0:T(8,128)(2,1)} all-reduce(f32[128,512]{1,0:T(8,128)S(1)} %fusion.6), channel_id=1, replica_groups=mesh['parts'=2,'feat'=8,'tok'=2] {'tok'}, use_global_device_ids=true, to_apply=%region_1.2 | all-reduce | flops 65536 | bytes 393216 | tf_op jit(solution)/shard_map/psum | solution.py:24
  110.9 0.0 all-gather.5.cloned.1.call-update
  110.9 1.5 constant_dynamic-slice_fusion
  112.4 0.0 reduce-scatter.2.cloned.1.call-done
  112.4 1.0 convert_element_type.7
  113.5 0.0 copy-start.2
  113.5 11.4 %fusion.2 = bf16[128,2,4096]{2,0,1:T(8,128)(2,1)} fusion(bf16[2,4096,896]{2,1,0:T(8,128)(2,1)} %param.11, bf16[128,896]{1,0:T(8,128)(2,1)S(1)} %convert_element_type.7), kind=kOutput, calls=%fused_computation.5 | convolution fusion | flops 1879048192 | bytes 17006592 | tf_op jit(solution)/shard_map/tj,qkj->qtk/dot_general | solution.py:27
  124.9 0.0 copy-done.2
  124.9 24.8 %all-gather.5.cloned.1.call-done = bf16[128,4096]{1,0:T(8,128)(2,1)} async-done(((bf16[128,512]{1,0:T(8,128)(2,1)}), bf16[128,4096]{1,0:T(8,128)(2,1)}) %all-gather.5.cloned.1.call-update) | async-done | bytes 1048592 | tf_op jit(solution)/shard_map/all_gather | solution.py:30
  149.7 6.5 %fusion = f32[128,1,2]{2,1,0:T(1,128)S(1)} fusion(bf16[128,2,4096]{2,0,1:T(8,128)(2,1)} %fusion.2, bf16[128,4096,1]{1,0,2:T(8,128)(2,1)} %bitcast.22), kind=kOutput, calls=%fused_computation.3 | convolution fusion | flops 2097152 | bytes 3146752 | tf_op jit(solution)/shard_map/tk,qtk->qt/dot_general | solution.py:28
  156.3 0.1 copy.11
  156.3 30.4 %psum.15 = f32[2,128]{1,0:T(2,128)} all-reduce(f32[2,128]{1,0:T(2,128)S(1)} %bitcast.21), channel_id=1, replica_groups=mesh['parts'=2,'feat'=8,'tok'=2] {'feat','tok'}, use_global_device_ids=true, to_apply=%region_2.3 | all-reduce | flops 256 | bytes 2048 | tf_op jit(solution)/shard_map/psum | solution.py:33
  (1 shorter events, 0.0 us)
Async XLA Ops:
  7.2 98.6 %copy-start = (bf16[2048,512]{1,0:T(8,128)(2,1)S(1)}, bf16[2048,512]{1,0:T(8,128)(2,1)}, u32[]{:S(2)}) copy-start(bf16[2048,512]{1,0:T(8,128)(2,1)} %param.10) | copy-start | bytes 6291460
  7.2 53.3 %all-gather.3.cloned.1.call-start = ((), (), s32[]{:S(2)}) async-start(), calls=%async_computation.1 | async-start | bytes 2064384 | tf_op jit(solution)/shard_map/all_gather | solution.py:12
  11.4 62.5 %copy-start.1 = (bf16[16,2048]{1,0:T(8,128)(2,1)S(1)}, bf16[16,2048]{1,0:T(8,128)(2,1)}, u32[]{:S(2)}) copy-start(bf16[16,2048]{1,0:T(8,128)(2,1)} %param.8) | copy-start | bytes 196612
  11.4 101.0 %reduce-scatter.2.cloned.1.call-start = ((), (), s32[]{:S(2)}) async-start(), calls=%async_computation.2 | async-start | bytes 1376256 | tf_op jit(solution)/shard_map/reduce_scatter | solution.py:16
  73.8 75.9 %all-gather.5.cloned.1.call-start = ((), (), s32[]{:S(2)}) async-start(), calls=%async_computation.3 | async-start | bytes 1179648 | tf_op jit(solution)/shard_map/all_gather | solution.py:30
  113.5 11.4 %copy-start.2 = (bf16[128,896]{1,0:T(8,128)(2,1)}, bf16[128,896]{1,0:T(8,128)(2,1)S(1)}, u32[]{:S(2)}) copy-start(bf16[128,896]{1,0:T(8,128)(2,1)S(1)} %convert_element_type.7) | copy-start | bytes 688132
Sparse Core Ops, SparseCore 0:
  11.5 48.9 all-gather.2
  73.9 7.4 reduce-scatter.1
  111.1 38.6 all-gather.4
where the time goes:
time: 194 us; the launch traced here: 193 us
  waiting for transfers between devices  73.9 us (38%)
  blocking collectives  66.3 us (34%)
  matrix products  31.7 us (16%)
  between operations  13.8 us (7%)
  local copies, waits for them, and re-layouts  4.03 us (2%)
  other arithmetic  3.37 us (2%)
    all_gather x1, waiting for transfers between devices, shards(): lax.all_gather(act, 'feat', axis=0, tiled=True)  49 us
    all_gather x1, blocking collectives, shards(): lax.all_gather(grads, 'feat', axis=0, tiled=True)  31.3 us
    psum x1, blocking collectives, shards(): scores = lax.psum(partial_value, ('feat', 'tok'))  30.4 us
    all_gather x1, waiting for transfers between devices, shards(): lax.all_gather(grad_block, 'feat', axis=1, tiled=True).astype(jnp.float32)  24.8 us
    dot_general x1, matrix products, shards(): jnp.dot(lax.all_gather(act, 'feat', axis=0, tiled=True), basis_in, prefer...  13.3 us
    dot_general x1, matrix products, shards(): jnp.einsum('tj,qkj->qtk', act_rot, precond, preferred_element_type=jnp.fl...  11.4 us
    dot_general x1, matrix products, shards(): jnp.einsum('tk,qtk->qt', lax.all_gather(grad_block, 'feat', axis=1, tiled...  6.53 us
    psum x1, blocking collectives, shards(): grad_block = lax.psum(grad_part, 'tok').astype(jnp.bfloat16)  4.68 us
  transfers between devices with their start and end apart: 3, of which 2 were waited for; matrix products, arithmetic and copies ran while one was open for 8% of the time, Pallas kernels for 0%

commit v1 on v0

v1 whole, which is shorter than its diff:
```python
import functools

import jax
import jax.numpy as jnp
from jax import lax
from jax.experimental import pallas as pl
from jax.experimental.pallas import tpu as pltpu
from jax.sharding import PartitionSpec as P

BF16 = jnp.bfloat16
F32 = jnp.float32
VMEM = pl.BlockSpec(memory_space=pltpu.VMEM)
LIMIT = 56 * 2**20


def call(kernel, outs, *args, scratch=(), flops=0, read=0):
    return pl.pallas_call(
        kernel,
        in_specs=[VMEM] * len(args),
        out_specs=[VMEM] * len(outs),
        out_shape=[jax.ShapeDtypeStruct(*o) for o in outs],
        scratch_shapes=list(scratch),
        compiler_params=pltpu.CompilerParams(vmem_limit_bytes=LIMIT),
        cost_estimate=pl.CostEstimate(flops=flops, bytes_accessed=read, transcendentals=0),
    )(*args)


def swap(x, axis, step):
    n = lax.axis_size(axis)
    return lax.ppermute(x, axis, [(i, i ^ step) for i in range(n)])


def select_kernel(order_ref, act_ref, grad_ref, act_out, grad_out):
    n = act_ref.shape[0]
    hot = (order_ref[...] == lax.broadcasted_iota(jnp.int32, (n, n), 1)).astype(BF16)
    act_out[...] = jnp.dot(hot, act_ref[...], preferred_element_type=F32).astype(BF16)
    grad_out[...] = jnp.dot(hot, grad_ref[...], preferred_element_type=F32).astype(BF16)


def halves(total, keep, give):
    half = total.shape[1] // 2
    low, high = total[:, :half], total[:, half:]
    first = lax.axis_index("tok") == 0
    keep[...] = jnp.where(first, low, high)
    give[...] = jnp.where(first, high, low)


def rotate_kernel(depth, *refs):
    *shards, basis, keep, give, rows, total = refs
    me = lax.axis_index("feat")
    n = shards[0].shape[0]
    for step, shard in enumerate(shards):
        rows[pl.ds(pl.multiple_of((me ^ step) * n, n), n), :] = shard[...]
    total[...] = jnp.zeros_like(total)

    def body(i, carry):
        at = pl.ds(pl.multiple_of(i * depth, depth), depth)
        total[...] += jnp.dot(rows[:, at], basis[at, :], preferred_element_type=F32)
        return carry

    lax.fori_loop(0, basis.shape[0] // depth, body, 0)
    halves(total, keep, give)


def rotate(shards, basis, depth):
    n, k = shards[0].shape
    tokens, width = n * len(shards), basis.shape[1]
    half = ((tokens, width // 2), F32)
    return call(
        functools.partial(rotate_kernel, depth), [half, half], *shards, basis,
        scratch=[pltpu.VMEM((tokens, k), BF16), pltpu.VMEM((tokens, width), F32)],
        flops=2 * tokens * k * width, read=k * width * 2,
    )


def add_kernel(a_ref, b_ref, out):
    out[...] = (a_ref[...] + b_ref[...]).astype(BF16)


def query_kernel(*refs):
    *blocks, precond, out = refs
    me, tok = lax.axis_index("feat"), lax.axis_index("tok")
    n = len(blocks) // 2
    w = blocks[0].shape[1]
    for q in range(precond.shape[0]):
        total = None
        for i, block in enumerate(blocks):
            owner = ((me ^ (i % n)) * 2 + (tok ^ (i // n))) * w
            part = precond[q, pl.ds(pl.multiple_of(owner, w), w), :]
            term = jnp.dot(block[...], part, preferred_element_type=F32)
            total = term if total is None else total + term
        out[q] = total


def score_kernel(mine, theirs, wide, act_rot, out):
    rot = (mine[...] + theirs[...]).astype(BF16)
    act_rot[...] = rot
    rot = rot.astype(F32)
    value = jnp.sum(wide[...] * rot[None], axis=2)
    for i in range(out.shape[0]):
        out[i] = value


def gather(x):
    n = lax.axis_size("feat")
    got = {0: x}
    far = sorted(range(2, n, 2), reverse=True)
    for step in far:
        got[step] = swap(x, "feat", step)
    got[1] = swap(x, "feat", 1)
    for step in far:
        got[step ^ 1] = swap(got[step], "feat", 1)
    return [got[i] for i in range(n)]


def shards(token_index, act_pool, grad_pool, basis_in, basis_out, precond):
    n = lax.axis_size("feat")
    stored, act_width = act_pool.shape
    tokens = stored * n
    act, grads = call(
        select_kernel, [(act_pool.shape, BF16), (grad_pool.shape, BF16)],
        token_index.reshape(-1, 1), act_pool, grad_pool,
    )
    grad_all = gather(grads)
    act_all = gather(act)
    keep, give = rotate(grad_all, basis_out, basis_out.shape[0] // 2)
    (grad_rot,) = call(add_kernel, [(keep.shape, BF16)], keep, swap(give, "tok", 1))
    blocks = gather(grad_rot)
    blocks += [swap(b, "tok", 1) for b in blocks]
    queries, _, width = precond.shape
    (wide,) = call(
        query_kernel, [((queries, tokens, width), F32)], *blocks, precond,
        flops=2 * tokens * precond.size, read=precond.size * 2,
    )
    keep, give = rotate(act_all, basis_in, act_width // 4)
    act_rot, parts = call(
        score_kernel, [(keep.shape, BF16), ((2 * n, queries, tokens), F32)],
        keep, swap(give, "tok", 1), wide,
    )
    scores = lax.all_to_all(parts, ("feat", "tok"), 0, 0, tiled=True).sum(axis=0)
    return scores, act_rot, grad_rot


def solution(mesh):
    placed = (
        P(("parts", "feat"), None),
        P(("parts", "feat"), "tok"),
        P(("parts", "feat"), "tok"),
        P(("parts", "tok"), "feat"),
        P(("parts", "tok"), "feat"),
        P("parts", None, ("feat", "tok")),
    )
    return jax.shard_map(
        shards,
        mesh=mesh,
        in_specs=placed,
        out_specs=(P("parts", None), P("parts", ("feat", "tok")), P("parts", ("feat", "tok"))),
        check_vma=False,
    )
```

time: 194 us -> 130 us (0.67)
  blocking collectives: 66.3 us -> 10.7 us
  Pallas kernels: 0 us -> 32.3 us
  matrix products: 31.7 us -> 0 us
  starting transfers between devices: 0.12 us -> 30.7 us
  waiting for transfers between devices: 73.9 us -> 48.5 us
  between operations: 13.8 us -> 0.9 us
  other arithmetic: 3.37 us -> 0.59 us
    all_gather x2 -> x0, waiting for transfers between devices: 73.8 us -> none  [the longest x1 49 us: shards(): lax.all_gather(act, 'feat', axis=0, tiled=True)]
    ppermute x0 -> x31, waiting for transfers between devices: none -> 48.5 us  [swap(): return lax.ppermute(x, axis, [(i, i ^ step) for i in range(n)])]
    psum x2 -> x0, blocking collectives: 35.1 us -> none  [the longest x1 30.4 us: shards(): scores = lax.psum(partial_value, ('feat', 'tok'))]
    pallas_call x0 -> x6, Pallas kernels: none -> 32.3 us  [call(): pl.pallas_call(kernel, in_specs=[VMEM] * len(args), out_specs=[VMEM] * le...]
    dot_general x4 -> x0, matrix products: 31.7 us -> none  [the longest x1 13.3 us: shards(): jnp.dot(lax.all_gather(act, 'feat', axis=0, tiled=True), basis_in, prefer...]
    all_gather x1 -> x0, blocking collectives: 31.3 us -> none  [shards(): lax.all_gather(grads, 'feat', axis=0, tiled=True)]
    ppermute x0 -> x31, starting transfers between devices: none -> 30.7 us  [swap(): return lax.ppermute(x, axis, [(i, i ^ step) for i in range(n)])]
    all_to_all x0 -> x1, blocking collectives: none -> 10.7 us  [shards(): lax.all_to_all(parts, ('feat', 'tok'), 0, 0, tiled=True).sum(axis=0)]
  transfers between devices with their start and end apart: 3 -> 31, of which waited for: 2 -> 15; matrix products, arithmetic and copies ran while one was open for 8% -> 0% of each run, Pallas kernels for 0% -> 22%
where the time goes in v1:
time: 130 us
  waiting for transfers between devices  48.5 us (37%)
  Pallas kernels  32.3 us (25%)
  starting transfers between devices  30.7 us (24%)
  blocking collectives  10.7 us (8%)
  local copies, waits for them, and re-layouts  5.87 us (5%)
    ppermute x31, waiting for transfers between devices, swap(): return lax.ppermute(x, axis, [(i, i ^ step) for i in range(n)])  48.5 us
    pallas_call x6, Pallas kernels, call(): pl.pallas_call(kernel, in_specs=[VMEM] * len(args), out_specs=[VMEM] * le...  32.3 us
    ppermute x31, starting transfers between devices, swap(): return lax.ppermute(x, axis, [(i, i ^ step) for i in range(n)])  30.7 us
    all_to_all x1, blocking collectives, shards(): lax.all_to_all(parts, ('feat', 'tok'), 0, 0, tiled=True).sum(axis=0)  10.7 us
    unnamed x62, local copies, waits for them, and re-layouts  4.55 us
  transfers between devices with their start and end apart: 31, of which 15 were waited for; matrix products, arithmetic and copies ran while one was open for 0% of the time, Pallas kernels for 22%

profile of v1, /device:TPU:0, one launch (start us, length us, event | category | flops | bytes accessed | tf_op | source)
XLA Modules:
  0.0 129.6 jit_solution(8378052266202921805)
XLA Ops:
  0.6 1.3 %copy.9.order_ref = s32[16,1]{1,0:T(8,128)} copy(s32[16,1]{0,1:T(1,128)} %bitcast.1) | data formatting | bytes 128 | tf_op jit(solution)/shard_map/reshape | solution.py:122
  2.0 1.9 %shard_map.85 = (bf16[16,7168]{1,0:T(8,128)(2,1)}, bf16[16,2048]{1,0:T(8,128)(2,1)}) custom-call(s32[16,1]{1,0:T(8,128)} %copy.9.order_ref, bf16[16,7168]{1,0:T(8,128)(2,1)} %act_ref.1, bf16[16,2048]{1,0:T(8,128)(2,1)} %grad_ref.1), custom_call_target="tpu_custom_call" | custom-call | tf_op jit(solution)/shard_map/pallas_call | solution.py:17
  3.9 3.0 %collective-permute-start.1 = (bf16[16,7168]{1,0:T(8,128)(2,1)}, bf16[16,7168]{1,0:T(8,128)(2,1)S(1)}, u32[]{:S(2)}, u32[]{:S(2)}) collective-permute-start(bf16[16,7168]{1,0:T(8,128)(2,1)} %get-tuple-element.11.refs_0_), channel_id=1, source_target_pairs={{0,4},{2,6},{4,0},{6,2},{8,12},{10,14},{12,8},{14,10},{1,5},{3,7},... | collective-permute-start | bytes 688136 | tf_op jit(solution)/shard_map/ppermute | solution.py:30
  6.9 2.6 %collective-permute-start.3 = (bf16[16,7168]{1,0:T(8,128)(2,1)}, bf16[16,7168]{1,0:T(8,128)(2,1)S(1)}, u32[]{:S(2)}, u32[]{:S(2)}) collective-permute-start(bf16[16,7168]{1,0:T(8,128)(2,1)} %get-tuple-element.11.refs_0_), channel_id=1, source_target_pairs={{0,8},{2,10},{4,12},{6,14},{8,0},{10,2},{12,4},{14,6},{1,9},{3,11}... | collective-permute-start | bytes 688136 | tf_op jit(solution)/shard_map/ppermute | solution.py:30
  9.5 1.7 %collective-permute-start.8 = (bf16[16,2048]{1,0:T(8,128)(2,1)}, bf16[16,2048]{1,0:T(8,128)(2,1)S(1)}, u32[]{:S(2)}, u32[]{:S(2)}) collective-permute-start(bf16[16,2048]{1,0:T(8,128)(2,1)} %get-tuple-element.14.refs_0_), channel_id=1, source_target_pairs={{0,2},{2,0},{4,6},{6,4},{8,10},{10,8},{12,14},{14,12},{1,3},{3,1},... | collective-permute-start | bytes 196616 | tf_op jit(solution)/shard_map/ppermute | solution.py:30
  11.9 2.1 %collective-permute-done.8.refs_1_ = bf16[16,2048]{1,0:T(8,128)(2,1)S(1)} collective-permute-done((bf16[16,2048]{1,0:T(8,128)(2,1)}, bf16[16,2048]{1,0:T(8,128)(2,1)S(1)}, u32[]{:S(2)}, u32[]{:S(2)}) %collective-permute-start.8) | collective-permute-done | bytes 65568 | tf_op jit(solution)/shard_map/ppermute | solution.py:30
  14.0 1.9 %collective-permute-start.11 = (bf16[16,2048]{1,0:T(8,128)(2,1)}, bf16[16,2048]{1,0:T(8,128)(2,1)S(1)}, u32[]{:S(2)}, u32[]{:S(2)}) collective-permute-start(bf16[16,2048]{1,0:T(8,128)(2,1)} %get-tuple-element.14.refs_0_), channel_id=1, source_target_pairs={{0,8},{2,10},{4,12},{6,14},{8,0},{10,2},{12,4},{14,6},{1,9},{3,11}... | collective-permute-start | bytes 196616 | tf_op jit(solution)/shard_map/ppermute | solution.py:30
  15.9 8.2 %collective-permute-done.9.refs_2_ = bf16[16,2048]{1,0:T(8,128)(2,1)S(1)} collective-permute-done((bf16[16,2048]{1,0:T(8,128)(2,1)}, bf16[16,2048]{1,0:T(8,128)(2,1)S(1)}, u32[]{:S(2)}, u32[]{:S(2)}) %collective-permute-start.9) | collective-permute-done | bytes 65568 | tf_op jit(solution)/shard_map/ppermute | solution.py:30
  24.1 2.4 %collective-permute-start.13 = (bf16[16,2048]{1,0:T(8,128)(2,1)}, bf16[16,2048]{1,0:T(8,128)(2,1)S(1)}, u32[]{:S(2)}, u32[]{:S(2)}) collective-permute-start(bf16[16,2048]{1,0:T(8,128)(2,1)} %get-tuple-element.14.refs_0_), channel_id=1, source_target_pairs={{0,12},{2,14},{4,8},{6,10},{8,4},{10,6},{12,0},{14,2},{1,13},{3,15... | collective-permute-start | bytes 196616 | tf_op jit(solution)/shard_map/ppermute | solution.py:30
  26.5 8.3 %collective-permute-done.11.refs_4_ = bf16[16,2048]{1,0:T(8,128)(2,1)S(1)} collective-permute-done((bf16[16,2048]{1,0:T(8,128)(2,1)}, bf16[16,2048]{1,0:T(8,128)(2,1)S(1)}, u32[]{:S(2)}, u32[]{:S(2)}) %collective-permute-start.11) | collective-permute-done | bytes 65568 | tf_op jit(solution)/shard_map/ppermute | solution.py:30
  34.8 1.5 %collective-permute-start = (bf16[16,7168]{1,0:T(8,128)(2,1)}, bf16[16,7168]{1,0:T(8,128)(2,1)S(1)}, u32[]{:S(2)}, u32[]{:S(2)}) collective-permute-start(bf16[16,7168]{1,0:T(8,128)(2,1)} %get-tuple-element.11.refs_0_), channel_id=1, source_target_pairs={{0,2},{2,0},{4,6},{6,4},{8,10},{10,8},{12,14},{14,12},{1,3},{3,1},... | collective-permute-start | bytes 688136 | tf_op jit(solution)/shard_map/ppermute | solution.py:30
  36.9 1.5 %collective-permute-start.4 = (bf16[16,7168]{1,0:T(8,128)(2,1)S(1)}, bf16[16,7168]{1,0:T(8,128)(2,1)S(1)}, u32[]{:S(2)}, u32[]{:S(2)}) collective-permute-start(bf16[16,7168]{1,0:T(8,128)(2,1)S(1)} %collective-permute-done.3.refs_4_), channel_id=1, source_target_pairs={{0,2},{2,0},{4,6},{6,4},{8,10},{10,8},{12,14},{14,12},{1,3},{3,1},... | collective-permute-start | bytes 688136 | tf_op jit(solution)/shard_map/ppermute | solution.py:30
  38.9 1.5 %collective-permute-start.10 = (bf16[16,2048]{1,0:T(8,128)(2,1)S(1)}, bf16[16,2048]{1,0:T(8,128)(2,1)S(1)}, u32[]{:S(2)}, u32[]{:S(2)}) collective-permute-start(bf16[16,2048]{1,0:T(8,128)(2,1)S(1)} %collective-permute-done.9.refs_2_), channel_id=1, source_target_pairs={{0,2},{2,0},{4,6},{6,4},{8,10},{10,8},{12,14},{14,12},{1,3},{3,1},... | collective-permute-start | bytes 196616 | tf_op jit(solution)/shard_map/ppermute | solution.py:30
  40.4 16.5 %collective-permute-done.10.refs_3_ = bf16[16,2048]{1,0:T(8,128)(2,1)S(1)} collective-permute-done((bf16[16,2048]{1,0:T(8,128)(2,1)S(1)}, bf16[16,2048]{1,0:T(8,128)(2,1)S(1)}, u32[]{:S(2)}, u32[]{:S(2)}) %collective-permute-start.10) | collective-permute-done | bytes 65568 | tf_op jit(solution)/shard_map/ppermute | solution.py:30
  56.9 1.5 %collective-permute-start.12 = (bf16[16,2048]{1,0:T(8,128)(2,1)S(1)}, bf16[16,2048]{1,0:T(8,128)(2,1)S(1)}, u32[]{:S(2)}, u32[]{:S(2)}) collective-permute-start(bf16[16,2048]{1,0:T(8,128)(2,1)S(1)} %collective-permute-done.11.refs_4_), channel_id=1, source_target_pairs={{0,2},{2,0},{4,6},{6,4},{8,10},{10,8},{12,14},{14,12},{1,3},{3,1},... | collective-permute-start | bytes 196616 | tf_op jit(solution)/shard_map/ppermute | solution.py:30
  58.5 2.7 %collective-permute-done.12.refs_5_ = bf16[16,2048]{1,0:T(8,128)(2,1)S(1)} collective-permute-done((bf16[16,2048]{1,0:T(8,128)(2,1)S(1)}, bf16[16,2048]{1,0:T(8,128)(2,1)S(1)}, u32[]{:S(2)}, u32[]{:S(2)}) %collective-permute-start.12) | collective-permute-done | bytes 65568 | tf_op jit(solution)/shard_map/ppermute | solution.py:30
  61.2 1.5 %collective-permute-start.14 = (bf16[16,2048]{1,0:T(8,128)(2,1)S(1)}, bf16[16,2048]{1,0:T(8,128)(2,1)S(1)}, u32[]{:S(2)}, u32[]{:S(2)}) collective-permute-start(bf16[16,2048]{1,0:T(8,128)(2,1)S(1)} %collective-permute-done.13.refs_6_), channel_id=1, source_target_pairs={{0,2},{2,0},{4,6},{6,4},{8,10},{10,8},{12,14},{14,12},{1,3},{3,1},... | collective-permute-start | bytes 196616 | tf_op jit(solution)/shard_map/ppermute | solution.py:30
  62.7 2.7 %collective-permute-done.14.refs_7_ = bf16[16,2048]{1,0:T(8,128)(2,1)S(1)} collective-permute-done((bf16[16,2048]{1,0:T(8,128)(2,1)S(1)}, bf16[16,2048]{1,0:T(8,128)(2,1)S(1)}, u32[]{:S(2)}, u32[]{:S(2)}) %collective-permute-start.14) | collective-permute-done | bytes 65568 | tf_op jit(solution)/shard_map/ppermute | solution.py:30
  66.1 3.3 %shard_map.87 = (f32[128,256]{1,0:T(8,128)}, f32[128,256]{1,0:T(8,128)}) custom-call(bf16[16,2048]{1,0:T(8,128)(2,1)} %get-tuple-element.14.refs_0_, bf16[16,2048]{1,0:T(8,128)(2,1)} %copy-done.24, bf16[16,2048]{1,0:T(8,128)(2,1)} %copy-done.25, bf16[16,2048]{1,0:T(8,128)(2,1)} %copy-done.28, bf16[16,2048]{1,0:T(8,128)(2,1)} %copy-done.26, ...), custom_call_target="tpu_custom_call" | custom-call | flops 268435456 | bytes 2097152 | tf_op jit(solution)/shard_map/pallas_call | solution.py:17
  71.0 14.3 %shard_map.86 = (f32[128,896]{1,0:T(8,128)}, f32[128,896]{1,0:T(8,128)}) custom-call(bf16[16,7168]{1,0:T(8,128)(2,1)} %get-tuple-element.11.refs_0_, bf16[16,7168]{1,0:T(8,128)(2,1)} %copy-done.4, bf16[16,7168]{1,0:T(8,128)(2,1)} %copy-done.1, bf16[16,7168]{1,0:T(8,128)(2,1)} %copy-done.5, bf16[16,7168]{1,0:T(8,128)(2,1)} %copy-done.2, ...), custom_call_target="tpu_custom_call" | custom-call | flops 3288334336 | bytes 25690112 | tf_op jit(solution)/shard_map/pallas_call | solution.py:17
  86.5 1.6 %shard_map.88.refs_0_ = bf16[128,256]{1,0:T(8,128)(2,1)} custom-call(f32[128,256]{1,0:T(8,128)} %get-tuple-element.15.a_ref, f32[128,256]{1,0:T(8,128)} %copy-done.8), custom_call_target="tpu_custom_call" | custom-call | tf_op jit(solution)/shard_map/pallas_call | solution.py:17
  88.1 1.5 %collective-permute-start.16 = (bf16[128,256]{1,0:T(8,128)(2,1)}, bf16[128,256]{1,0:T(8,128)(2,1)S(1)}, u32[]{:S(2)}, u32[]{:S(2)}) collective-permute-start(bf16[128,256]{1,0:T(8,128)(2,1)} %shard_map.88.refs_0_), channel_id=1, source_target_pairs={{0,2},{2,0},{4,6},{6,4},{8,10},{10,8},{12,14},{14,12},{1,3},{3,1},... | collective-permute-start | bytes 196616 | tf_op jit(solution)/shard_map/ppermute | solution.py:30
  89.6 3.1 %collective-permute-start.19 = (bf16[128,256]{1,0:T(8,128)(2,1)}, bf16[128,256]{1,0:T(8,128)(2,1)S(1)}, u32[]{:S(2)}, u32[]{:S(2)}) collective-permute-start(bf16[128,256]{1,0:T(8,128)(2,1)} %shard_map.88.refs_0_), channel_id=1, source_target_pairs={{0,8},{2,10},{4,12},{6,14},{8,0},{10,2},{12,4},{14,6},{1,9},{3,11}... | collective-permute-start | bytes 196616 | tf_op jit(solution)/shard_map/ppermute | solution.py:30
  92.7 1.3 %collective-permute-start.21 = (bf16[128,256]{1,0:T(8,128)(2,1)}, bf16[128,256]{1,0:T(8,128)(2,1)S(1)}, u32[]{:S(2)}, u32[]{:S(2)}) collective-permute-start(bf16[128,256]{1,0:T(8,128)(2,1)} %shard_map.88.refs_0_), channel_id=1, source_target_pairs={{0,12},{2,14},{4,8},{6,10},{8,4},{10,6},{12,0},{14,2},{1,13},{3,15... | collective-permute-start | bytes 196616 | tf_op jit(solution)/shard_map/ppermute | solution.py:30
  95.2 2.6 %collective-permute-done.19.refs_4_ = bf16[128,256]{1,0:T(8,128)(2,1)S(1)} collective-permute-done((bf16[128,256]{1,0:T(8,128)(2,1)}, bf16[128,256]{1,0:T(8,128)(2,1)S(1)}, u32[]{:S(2)}, u32[]{:S(2)}) %collective-permute-start.19) | collective-permute-done | bytes 65568 | tf_op jit(solution)/shard_map/ppermute | solution.py:30
  99.0 0.8 collective-permute-start.22
  100.3 1.7 %collective-permute-done.20.refs_5_ = bf16[128,256]{1,0:T(8,128)(2,1)S(1)} collective-permute-done((bf16[128,256]{1,0:T(8,128)(2,1)S(1)}, bf16[128,256]{1,0:T(8,128)(2,1)S(1)}, u32[]{:S(2)}, u32[]{:S(2)}) %collective-permute-start.20) | collective-permute-done | bytes 65568 | tf_op jit(solution)/shard_map/ppermute | solution.py:30
  102.1 1.2 collective-permute-done.22.refs_7_
  106.3 8.9 %shard_map.89.wide = f32[2,128,896]{2,1,0:T(8,128)} custom-call(bf16[128,256]{1,0:T(8,128)(2,1)} %shard_map.88.refs_0_, bf16[128,256]{1,0:T(8,128)(2,1)} %copy-done.9, bf16[128,256]{1,0:T(8,128)(2,1)} %copy-done.10, bf16[128,256]{1,0:T(8,128)(2,1)} %copy-done.14, bf16[128,256]{1,0:T(8,128)(2,1)} %copy-done.11, bf16[128,256]{1,0:T(8,128)(2,1)} %copy-done.15, ...), custom_call_target="tpu_custom_call" | custom-call | flops 1879048192 | bytes 14680064 | tf_op jit(solution)/shard_map/pallas_call | solution.py:17
  115.3 0.8 copy-done
  116.0 2.2 %shard_map.90 = (bf16[128,896]{1,0:T(8,128)(2,1)}, f32[16,2,128]{2,1,0:T(2,128)}) custom-call(f32[128,896]{1,0:T(8,128)} %get-tuple-element.12.mine, f32[128,896]{1,0:T(8,128)} %copy-done, f32[2,128,896]{2,1,0:T(8,128)} %shard_map.89.wide), custom_call_target="tpu_custom_call" | custom-call | tf_op jit(solution)/shard_map/pallas_call | solution.py:17
  118.3 10.7 %all_to_all.5 = f32[16,2,128]{2,1,0:T(2,128)S(1)} all-to-all(f32[16,2,128]{2,1,0:T(2,128)} %get-tuple-element.17), channel_id=1, replica_groups=mesh['parts'=2,'feat'=8,'tok'=2] {'feat','tok'}, dimensions={0} | all-to-all | bytes 32768 | tf_op jit(solution)/shard_map/all_to_all | solution.py:140
  (101 shorter events, 11.4 us)
Async XLA Ops:
  3.9 32.5 %collective-permute-start.1 = (bf16[16,7168]{1,0:T(8,128)(2,1)}, bf16[16,7168]{1,0:T(8,128)(2,1)S(1)}, u32[]{:S(2)}, u32[]{:S(2)}) collective-permute-start(bf16[16,7168]{1,0:T(8,128)(2,1)} %get-tuple-element.11.refs_0_), channel_id=1, source_target_pairs={{0,4},{2,6},{4,0},{6,2},{8,12},{10,14},{12,8},{14,10},{1,5},{3,7},... | collective-permute-start | bytes 688136 | tf_op jit(solution)/shard_map/ppermute | solution.py:30
  6.9 29.9 %collective-permute-start.3 = (bf16[16,7168]{1,0:T(8,128)(2,1)}, bf16[16,7168]{1,0:T(8,128)(2,1)S(1)}, u32[]{:S(2)}, u32[]{:S(2)}) collective-permute-start(bf16[16,7168]{1,0:T(8,128)(2,1)} %get-tuple-element.11.refs_0_), channel_id=1, source_target_pairs={{0,8},{2,10},{4,12},{6,14},{8,0},{10,2},{12,4},{14,6},{1,9},{3,11}... | collective-permute-start | bytes 688136 | tf_op jit(solution)/shard_map/ppermute | solution.py:30
  9.5 28.9 %collective-permute-start.5 = (bf16[16,7168]{1,0:T(8,128)(2,1)}, bf16[16,7168]{1,0:T(8,128)(2,1)S(1)}, u32[]{:S(2)}, u32[]{:S(2)}) collective-permute-start(bf16[16,7168]{1,0:T(8,128)(2,1)} %get-tuple-element.11.refs_0_), channel_id=1, source_target_pairs={{0,12},{2,14},{4,8},{6,10},{8,4},{10,6},{12,0},{14,2},{1,13},{3,15... | collective-permute-start | bytes 688136 | tf_op jit(solution)/shard_map/ppermute | solution.py:30
  9.5 4.5 %collective-permute-start.8 = (bf16[16,2048]{1,0:T(8,128)(2,1)}, bf16[16,2048]{1,0:T(8,128)(2,1)S(1)}, u32[]{:S(2)}, u32[]{:S(2)}) collective-permute-start(bf16[16,2048]{1,0:T(8,128)(2,1)} %get-tuple-element.14.refs_0_), channel_id=1, source_target_pairs={{0,2},{2,0},{4,6},{6,4},{8,10},{10,8},{12,14},{14,12},{1,3},{3,1},... | collective-permute-start | bytes 196616 | tf_op jit(solution)/shard_map/ppermute | solution.py:30
  11.2 12.9 %collective-permute-start.9 = (bf16[16,2048]{1,0:T(8,128)(2,1)}, bf16[16,2048]{1,0:T(8,128)(2,1)S(1)}, u32[]{:S(2)}, u32[]{:S(2)}) collective-permute-start(bf16[16,2048]{1,0:T(8,128)(2,1)} %get-tuple-element.14.refs_0_), channel_id=1, source_target_pairs={{0,4},{2,6},{4,0},{6,2},{8,12},{10,14},{12,8},{14,10},{1,5},{3,7},... | collective-permute-start | bytes 196616 | tf_op jit(solution)/shard_map/ppermute | solution.py:30
  14.0 51.5 %copy-start.24 = (bf16[16,2048]{1,0:T(8,128)(2,1)}, bf16[16,2048]{1,0:T(8,128)(2,1)S(1)}, u32[]{:S(2)}) copy-start(bf16[16,2048]{1,0:T(8,128)(2,1)S(1)} %collective-permute-done.8.refs_1_) | copy-start | bytes 196612
  14.0 20.8 %collective-permute-start.11 = (bf16[16,2048]{1,0:T(8,128)(2,1)}, bf16[16,2048]{1,0:T(8,128)(2,1)S(1)}, u32[]{:S(2)}, u32[]{:S(2)}) collective-permute-start(bf16[16,2048]{1,0:T(8,128)(2,1)} %get-tuple-element.14.refs_0_), channel_id=1, source_target_pairs={{0,8},{2,10},{4,12},{6,14},{8,0},{10,2},{12,4},{14,6},{1,9},{3,11}... | collective-permute-start | bytes 196616 | tf_op jit(solution)/shard_map/ppermute | solution.py:30
  24.1 14.8 %collective-permute-start.13 = (bf16[16,2048]{1,0:T(8,128)(2,1)}, bf16[16,2048]{1,0:T(8,128)(2,1)S(1)}, u32[]{:S(2)}, u32[]{:S(2)}) collective-permute-start(bf16[16,2048]{1,0:T(8,128)(2,1)} %get-tuple-element.14.refs_0_), channel_id=1, source_target_pairs={{0,12},{2,14},{4,8},{6,10},{8,4},{10,6},{12,0},{14,2},{1,13},{3,15... | collective-permute-start | bytes 196616 | tf_op jit(solution)/shard_map/ppermute | solution.py:30
  34.8 34.6 %collective-permute-start = (bf16[16,7168]{1,0:T(8,128)(2,1)}, bf16[16,7168]{1,0:T(8,128)(2,1)S(1)}, u32[]{:S(2)}, u32[]{:S(2)}) collective-permute-start(bf16[16,7168]{1,0:T(8,128)(2,1)} %get-tuple-element.11.refs_0_), channel_id=1, source_target_pairs={{0,2},{2,0},{4,6},{6,4},{8,10},{10,8},{12,14},{14,12},{1,3},{3,1},... | collective-permute-start | bytes 688136 | tf_op jit(solution)/shard_map/ppermute | solution.py:30
  36.3 33.1 %collective-permute-start.2 = (bf16[16,7168]{1,0:T(8,128)(2,1)S(1)}, bf16[16,7168]{1,0:T(8,128)(2,1)S(1)}, u32[]{:S(2)}, u32[]{:S(2)}) collective-permute-start(bf16[16,7168]{1,0:T(8,128)(2,1)S(1)} %collective-permute-done.1.refs_2_), channel_id=1, source_target_pairs={{0,2},{2,0},{4,6},{6,4},{8,10},{10,8},{12,14},{14,12},{1,3},{3,1},... | collective-permute-start | bytes 688136 | tf_op jit(solution)/shard_map/ppermute | solution.py:30
  36.9 32.6 %collective-permute-start.4 = (bf16[16,7168]{1,0:T(8,128)(2,1)S(1)}, bf16[16,7168]{1,0:T(8,128)(2,1)S(1)}, u32[]{:S(2)}, u32[]{:S(2)}) collective-permute-start(bf16[16,7168]{1,0:T(8,128)(2,1)S(1)} %collective-permute-done.3.refs_4_), channel_id=1, source_target_pairs={{0,2},{2,0},{4,6},{6,4},{8,10},{10,8},{12,14},{14,12},{1,3},{3,1},... | collective-permute-start | bytes 688136 | tf_op jit(solution)/shard_map/ppermute | solution.py:30
  38.4 31.1 %collective-permute-start.6 = (bf16[16,7168]{1,0:T(8,128)(2,1)S(1)}, bf16[16,7168]{1,0:T(8,128)(2,1)S(1)}, u32[]{:S(2)}, u32[]{:S(2)}) collective-permute-start(bf16[16,7168]{1,0:T(8,128)(2,1)S(1)} %collective-permute-done.5.refs_6_), channel_id=1, source_target_pairs={{0,2},{2,0},{4,6},{6,4},{8,10},{10,8},{12,14},{14,12},{1,3},{3,1},... | collective-permute-start | bytes 688136 | tf_op jit(solution)/shard_map/ppermute | solution.py:30
  38.9 18.1 %collective-permute-start.10 = (bf16[16,2048]{1,0:T(8,128)(2,1)S(1)}, bf16[16,2048]{1,0:T(8,128)(2,1)S(1)}, u32[]{:S(2)}, u32[]{:S(2)}) collective-permute-start(bf16[16,2048]{1,0:T(8,128)(2,1)S(1)} %collective-permute-done.9.refs_2_), channel_id=1, source_target_pairs={{0,2},{2,0},{4,6},{6,4},{8,10},{10,8},{12,14},{14,12},{1,3},{3,1},... | collective-permute-start | bytes 196616 | tf_op jit(solution)/shard_map/ppermute | solution.py:30
  56.9 4.3 %collective-permute-start.12 = (bf16[16,2048]{1,0:T(8,128)(2,1)S(1)}, bf16[16,2048]{1,0:T(8,128)(2,1)S(1)}, u32[]{:S(2)}, u32[]{:S(2)}) collective-permute-start(bf16[16,2048]{1,0:T(8,128)(2,1)S(1)} %collective-permute-done.11.refs_4_), channel_id=1, source_target_pairs={{0,2},{2,0},{4,6},{6,4},{8,10},{10,8},{12,14},{14,12},{1,3},{3,1},... | collective-permute-start | bytes 196616 | tf_op jit(solution)/shard_map/ppermute | solution.py:30
  61.2 4.3 %collective-permute-start.14 = (bf16[16,2048]{1,0:T(8,128)(2,1)S(1)}, bf16[16,2048]{1,0:T(8,128)(2,1)S(1)}, u32[]{:S(2)}, u32[]{:S(2)}) collective-permute-start(bf16[16,2048]{1,0:T(8,128)(2,1)S(1)} %collective-permute-done.13.refs_6_), channel_id=1, source_target_pairs={{0,2},{2,0},{4,6},{6,4},{8,10},{10,8},{12,14},{14,12},{1,3},{3,1},... | collective-permute-start | bytes 196616 | tf_op jit(solution)/shard_map/ppermute | solution.py:30
  69.4 16.4 %collective-permute-start.15 = (f32[128,256]{1,0:T(8,128)}, f32[128,256]{1,0:T(8,128)S(1)}, u32[]{:S(2)}, u32[]{:S(2)}) collective-permute-start(f32[128,256]{1,0:T(8,128)} %get-tuple-element.16), channel_id=1, source_target_pairs={{0,1},{1,0},{2,3},{3,2},{4,5},{5,4},{6,7},{7,6},{8,9},{9,8},{10,11... | collective-permute-start | bytes 393224 | tf_op jit(solution)/shard_map/ppermute | solution.py:30
  85.3 30.0 %collective-permute-start.7 = (f32[128,896]{1,0:T(8,128)}, f32[128,896]{1,0:T(8,128)S(1)}, u32[]{:S(2)}, u32[]{:S(2)}) collective-permute-start(f32[128,896]{1,0:T(8,128)} %get-tuple-element.13), channel_id=1, source_target_pairs={{0,1},{1,0},{2,3},{3,2},{4,5},{5,4},{6,7},{7,6},{8,9},{9,8},{10,11... | collective-permute-start | bytes 1376264 | tf_op jit(solution)/shard_map/ppermute | solution.py:30
  88.1 5.9 %collective-permute-start.16 = (bf16[128,256]{1,0:T(8,128)(2,1)}, bf16[128,256]{1,0:T(8,128)(2,1)S(1)}, u32[]{:S(2)}, u32[]{:S(2)}) collective-permute-start(bf16[128,256]{1,0:T(8,128)(2,1)} %shard_map.88.refs_0_), channel_id=1, source_target_pairs={{0,2},{2,0},{4,6},{6,4},{8,10},{10,8},{12,14},{14,12},{1,3},{3,1},... | collective-permute-start | bytes 196616 | tf_op jit(solution)/shard_map/ppermute | solution.py:30
  89.6 5.1 %collective-permute-start.17 = (bf16[128,256]{1,0:T(8,128)(2,1)}, bf16[128,256]{1,0:T(8,128)(2,1)S(1)}, u32[]{:S(2)}, u32[]{:S(2)}) collective-permute-start(bf16[128,256]{1,0:T(8,128)(2,1)} %shard_map.88.refs_0_), channel_id=1, source_target_pairs={{0,4},{2,6},{4,0},{6,2},{8,12},{10,14},{12,8},{14,10},{1,5},{3,7},... | collective-permute-start | bytes 196616 | tf_op jit(solution)/shard_map/ppermute | solution.py:30
  89.6 8.2 %collective-permute-start.19 = (bf16[128,256]{1,0:T(8,128)(2,1)}, bf16[128,256]{1,0:T(8,128)(2,1)S(1)}, u32[]{:S(2)}, u32[]{:S(2)}) collective-permute-start(bf16[128,256]{1,0:T(8,128)(2,1)} %shard_map.88.refs_0_), channel_id=1, source_target_pairs={{0,8},{2,10},{4,12},{6,14},{8,0},{10,2},{12,4},{14,6},{1,9},{3,11}... | collective-permute-start | bytes 196616 | tf_op jit(solution)/shard_map/ppermute | solution.py:30
  92.7 6.4 %collective-permute-start.21 = (bf16[128,256]{1,0:T(8,128)(2,1)}, bf16[128,256]{1,0:T(8,128)(2,1)S(1)}, u32[]{:S(2)}, u32[]{:S(2)}) collective-permute-start(bf16[128,256]{1,0:T(8,128)(2,1)} %shard_map.88.refs_0_), channel_id=1, source_target_pairs={{0,12},{2,14},{4,8},{6,10},{8,4},{10,6},{12,0},{14,2},{1,13},{3,15... | collective-permute-start | bytes 196616 | tf_op jit(solution)/shard_map/ppermute | solution.py:30
  94.0 5.8 %collective-permute-start.23 = (bf16[128,256]{1,0:T(8,128)(2,1)}, bf16[128,256]{1,0:T(8,128)(2,1)S(1)}, u32[]{:S(2)}, u32[]{:S(2)}) collective-permute-start(bf16[128,256]{1,0:T(8,128)(2,1)} %shard_map.88.refs_0_), channel_id=1, source_target_pairs={{0,1},{1,0},{2,3},{3,2},{4,5},{5,4},{6,7},{7,6},{8,9},{9,8},{10,11... | collective-permute-start | bytes 196616 | tf_op jit(solution)/shard_map/ppermute | solution.py:30
  94.7 5.2 %collective-permute-start.18 = (bf16[128,256]{1,0:T(8,128)(2,1)S(1)}, bf16[128,256]{1,0:T(8,128)(2,1)S(1)}, u32[]{:S(2)}, u32[]{:S(2)}) collective-permute-start(bf16[128,256]{1,0:T(8,128)(2,1)S(1)} %collective-permute-done.17.refs_2_), channel_id=1, source_target_pairs={{0,2},{2,0},{4,6},{6,4},{8,10},{10,8},{12,14},{14,12},{1,3},{3,1},... | collective-permute-start | bytes 196616 | tf_op jit(solution)/shard_map/ppermute | solution.py:30
  97.8 4.3 %collective-permute-start.20 = (bf16[128,256]{1,0:T(8,128)(2,1)S(1)}, bf16[128,256]{1,0:T(8,128)(2,1)S(1)}, u32[]{:S(2)}, u32[]{:S(2)}) collective-permute-start(bf16[128,256]{1,0:T(8,128)(2,1)S(1)} %collective-permute-done.19.refs_4_), channel_id=1, source_target_pairs={{0,2},{2,0},{4,6},{6,4},{8,10},{10,8},{12,14},{14,12},{1,3},{3,1},... | collective-permute-start | bytes 196616 | tf_op jit(solution)/shard_map/ppermute | solution.py:30
  99.0 4.3 %collective-permute-start.22 = (bf16[128,256]{1,0:T(8,128)(2,1)S(1)}, bf16[128,256]{1,0:T(8,128)(2,1)S(1)}, u32[]{:S(2)}, u32[]{:S(2)}) collective-permute-start(bf16[128,256]{1,0:T(8,128)(2,1)S(1)} %collective-permute-done.21.refs_6_), channel_id=1, source_target_pairs={{0,2},{2,0},{4,6},{6,4},{8,10},{10,8},{12,14},{14,12},{1,3},{3,1},... | collective-permute-start | bytes 196616 | tf_op jit(solution)/shard_map/ppermute | solution.py:30
  99.8 3.5 %collective-permute-start.24 = (bf16[128,256]{1,0:T(8,128)(2,1)S(1)}, bf16[128,256]{1,0:T(8,128)(2,1)S(1)}, u32[]{:S(2)}, u32[]{:S(2)}) collective-permute-start(bf16[128,256]{1,0:T(8,128)(2,1)S(1)} %collective-permute-done.16.refs_1_), channel_id=1, source_target_pairs={{0,1},{1,0},{2,3},{3,2},{4,5},{5,4},{6,7},{7,6},{8,9},{9,8},{10,11... | collective-permute-start | bytes 196616 | tf_op jit(solution)/shard_map/ppermute | solution.py:30
  99.8 4.0 %collective-permute-start.25 = (bf16[128,256]{1,0:T(8,128)(2,1)S(1)}, bf16[128,256]{1,0:T(8,128)(2,1)S(1)}, u32[]{:S(2)}, u32[]{:S(2)}) collective-permute-start(bf16[128,256]{1,0:T(8,128)(2,1)S(1)} %collective-permute-done.17.refs_2_), channel_id=1, source_target_pairs={{0,1},{1,0},{2,3},{3,2},{4,5},{5,4},{6,7},{7,6},{8,9},{9,8},{10,11... | collective-permute-start | bytes 196616 | tf_op jit(solution)/shard_map/ppermute | solution.py:30
  102.1 1.9 %collective-permute-start.27 = (bf16[128,256]{1,0:T(8,128)(2,1)S(1)}, bf16[128,256]{1,0:T(8,128)(2,1)S(1)}, u32[]{:S(2)}, u32[]{:S(2)}) collective-permute-start(bf16[128,256]{1,0:T(8,128)(2,1)S(1)} %collective-permute-done.19.refs_4_), channel_id=1, source_target_pairs={{0,1},{1,0},{2,3},{3,2},{4,5},{5,4},{6,7},{7,6},{8,9},{9,8},{10,11... | collective-permute-start | bytes 196616 | tf_op jit(solution)/shard_map/ppermute | solution.py:30
  103.3 1.3 collective-permute-start.29
  103.3 1.4 %collective-permute-start.26 = (bf16[128,256]{1,0:T(8,128)(2,1)S(1)}, bf16[128,256]{1,0:T(8,128)(2,1)S(1)}, u32[]{:S(2)}, u32[]{:S(2)}) collective-permute-start(bf16[128,256]{1,0:T(8,128)(2,1)S(1)} %collective-permute-done.18.refs_3_), channel_id=1, source_target_pairs={{0,1},{1,0},{2,3},{3,2},{4,5},{5,4},{6,7},{7,6},{8,9},{9,8},{10,11... | collective-permute-start | bytes 196616 | tf_op jit(solution)/shard_map/ppermute | solution.py:30
  103.8 1.3 collective-permute-start.28
  103.9 1.3 %collective-permute-start.30 = (bf16[128,256]{1,0:T(8,128)(2,1)S(1)}, bf16[128,256]{1,0:T(8,128)(2,1)S(1)}, u32[]{:S(2)}, u32[]{:S(2)}) collective-permute-start(bf16[128,256]{1,0:T(8,128)(2,1)S(1)} %collective-permute-done.22.refs_7_), channel_id=1, source_target_pairs={{0,1},{1,0},{2,3},{3,2},{4,5},{5,4},{6,7},{7,6},{8,9},{9,8},{10,11... | collective-permute-start | bytes 196616 | tf_op jit(solution)/shard_map/ppermute | solution.py:30
  (30 other events, 272.6 us)

commit v2 on v1

v2 whole, which is shorter than its diff:
```python
import functools
import math

import jax
import jax.numpy as jnp
from jax import lax
from jax.experimental import pallas as pl
from jax.experimental.pallas import tpu as pltpu
from jax.sharding import PartitionSpec as P

BF16 = jnp.bfloat16
F32 = jnp.float32
VMEM = pl.BlockSpec(memory_space=pltpu.VMEM)
ANY = pl.BlockSpec(memory_space=pl.ANY)
ROOM = 4 * 2**20


def call(kernel, outs, *args, scratch=(), flops=0, read=0, specs=None):
    held = [(s.shape, s.dtype) for s in scratch if hasattr(s, "inner_aval")] + list(outs)
    held = sum(math.prod(shape) * jnp.dtype(dtype).itemsize for shape, dtype in held)
    return pl.pallas_call(
        kernel,
        in_specs=specs or [VMEM] * len(args),
        out_specs=[VMEM] * len(outs),
        out_shape=[jax.ShapeDtypeStruct(*o) for o in outs],
        scratch_shapes=list(scratch),
        compiler_params=pltpu.CompilerParams(vmem_limit_bytes=ROOM + held),
        cost_estimate=pl.CostEstimate(flops=flops, bytes_accessed=read, transcendentals=0),
    )(*args)


def swap(x, axis, step):
    n = lax.axis_size(axis)
    return lax.ppermute(x, axis, [(i, i ^ step) for i in range(n)])


def pick(order_ref, pool):
    n = pool.shape[0]
    hot = (order_ref[...] == lax.broadcasted_iota(jnp.int32, (n, n), 0)).astype(BF16)
    rows = lax.dot_general(hot, pool[...], (((0,), (0,)), ((), ())), preferred_element_type=F32)
    return rows.astype(BF16)


def select_kernel(order_ref, pool, out, order_in, pool_in, order_sem, pool_sem):
    first = pltpu.make_async_copy(order_ref, order_in, order_sem)
    second = pltpu.make_async_copy(pool, pool_in, pool_sem)
    first.start()
    second.start()
    first.wait()
    second.wait()
    out[...] = pick(order_in, pool_in)


def select_bundle_kernel(order_ref, pool, *refs):
    *near, out, bundle = refs
    for i, shard in enumerate(near):
        bundle[i] = shard[...]
    out[...] = pick(order_ref, pool)


def halves(total, keep, give):
    half = total.shape[1] // 2
    low, high = total[:, :half], total[:, half:]
    first = lax.axis_index("tok") == 0
    keep[...] = jnp.where(first, low, high)
    give[...] = jnp.where(first, high, low)


def bundle_kernel(count, *refs):
    out = refs[-1]
    for i in range(count):
        out[i] = refs[i][...]


def bundle(xs, deps=()):
    (out,) = call(
        functools.partial(bundle_kernel, len(xs)), [((len(xs),) + xs[0].shape, xs[0].dtype)],
        *xs, *deps, specs=[VMEM] * len(xs) + [ANY] * len(deps),
    )
    return out


def rotate_kernel(depth, near, far, *refs):
    near, refs = refs[:near], refs[near:]
    far, (basis, keep, give, rows, total) = refs[:far], refs[far:]
    me = lax.axis_index("feat")
    n = near[0].shape[0]
    far = [one.at[i] for one in far for i in range(one.shape[0])]
    for i, (mine, other) in enumerate(zip(near, far)):
        rows[pl.ds(pl.multiple_of((me ^ (2 * i)) * n, n), n), :] = mine[...]
        rows[pl.ds(pl.multiple_of((me ^ (2 * i + 1)) * n, n), n), :] = other[...]
    total[...] = jnp.zeros_like(total)

    def body(i, carry):
        at = pl.ds(pl.multiple_of(i * depth, depth), depth)
        total[...] += jnp.dot(rows[:, at], basis[at, :], preferred_element_type=F32)
        return carry

    lax.fori_loop(0, basis.shape[0] // depth, body, 0)
    halves(total, keep, give)


def rotate(near, far, basis, depth, flops):
    n, k = near[0].shape
    tokens, width = 2 * n * len(near), basis.shape[1]
    half = ((tokens, width // 2), F32)
    return call(
        functools.partial(rotate_kernel, depth, len(near), len(far)), [half, half], *near, *far, basis,
        scratch=[pltpu.VMEM((tokens, k), BF16), pltpu.VMEM((tokens, width), F32)],
        flops=flops, read=k * width * 2,
    )


def add_kernel(a_ref, b_ref, out, again):
    total = (a_ref[...] + b_ref[...]).astype(BF16)
    out[...] = total
    again[...] = total


def query_kernel(*refs):
    *blocks, precond, out = refs
    me, tok = lax.axis_index("feat"), lax.axis_index("tok")
    count, _, w = blocks[0].shape
    for q in range(precond.shape[0]):
        total = None
        for i, block in enumerate(blocks):
            for j in range(count):
                owner = ((me ^ (2 * j + i % 2)) * 2 + (tok ^ (i // 2))) * w
                part = precond[q, pl.ds(pl.multiple_of(owner, w), w), :]
                term = jnp.dot(block[j], part, preferred_element_type=F32)
                total = term if total is None else total + term
        out[q] = total


def score_kernel(mine, theirs, wide, act_rot, out):
    rot = (mine[...] + theirs[...]).astype(BF16)
    act_rot[...] = rot
    rot = rot.astype(F32)
    value = jnp.sum(wide[...] * rot[None], axis=2)
    for i in range(out.shape[0]):
        out[i] = value


def across(x):
    return [x] + [swap(x, "feat", step) for step in range(2, lax.axis_size("feat"), 2)]


def after(x, *deps):
    return lax.optimization_barrier((x,) + deps)[0]


def shards(token_index, act_pool, grad_pool, basis_in, basis_out, precond):
    n = lax.axis_size("feat")
    stored, act_width = act_pool.shape
    tokens = stored * n
    (grads,) = call(
        select_kernel, [(grad_pool.shape, BF16)], token_index, grad_pool,
        specs=[ANY, ANY], flops=4000 * basis_out.size,
        scratch=[
            pltpu.VMEM(token_index.shape, jnp.int32), pltpu.VMEM(grad_pool.shape, BF16),
            pltpu.SemaphoreType.DMA, pltpu.SemaphoreType.DMA,
        ],
    )
    near = across(grads)
    act, near_bundle = call(
        select_bundle_kernel, [(act_pool.shape, BF16), ((n // 2,) + grads.shape, BF16)],
        token_index, act_pool, *near, flops=800 * basis_in.size,
    )
    act_near = across(act)
    keep, give = rotate(near, [swap(near_bundle, "feat", 1)], basis_out, basis_out.shape[0] // 2, 800 * precond.size)
    half = len(act_near) // 2
    act_far = [swap(bundle(act_near[:half]), "feat", 1)]
    grad_rot, block = call(add_kernel, [(keep.shape, BF16)] * 2, keep, swap(give, "tok", 1))
    act_far += [swap(bundle(act_near[half:], [block]), "feat", 1)]
    mine = bundle(across(block))
    other = swap(mine, "feat", 1)
    blocks = [mine, other, swap(mine, "tok", 1), swap(other, "tok", 1)]
    queries, _, width = precond.shape
    (wide,) = call(
        query_kernel, [((queries, tokens, width), F32)], *blocks, precond,
        flops=2 * tokens * precond.size, read=precond.size * 2,
    )
    act_near[0] = after(act_near[0], mine)
    keep, give = rotate(act_near, act_far, basis_in, act_width // 4, 1600 * precond.size)
    act_rot, parts = call(
        score_kernel, [(keep.shape, BF16), ((2 * n, queries, tokens), F32)],
        keep, swap(give, "tok", 1), wide,
    )
    scores = lax.all_to_all(parts, ("feat", "tok"), 0, 0, tiled=True).sum(axis=0)
    return scores, act_rot, grad_rot


def solution(mesh):
    placed = (
        P(("parts", "feat"), None),
        P(("parts", "feat"), "tok"),
        P(("parts", "feat"), "tok"),
        P(("parts", "tok"), "feat"),
        P(("parts", "tok"), "feat"),
        P("parts", None, ("feat", "tok")),
    )
    return jax.shard_map(
        shards,
        mesh=mesh,
        in_specs=placed,
        out_specs=(P("parts", None), P("parts", ("feat", "tok")), P("parts", ("feat", "tok"))),
        check_vma=False,
    )
```

time: 130 us -> 71.7 us (0.55)
  waiting for transfers between devices: 48.5 us -> 25.4 us
  Pallas kernels: 32.3 us -> 9.44 us
  starting transfers between devices: 30.7 us -> 20.9 us
  local copies, waits for them, and re-layouts: 5.87 us -> 1.59 us
  blocking collectives: 10.7 us -> 12.7 us
    ppermute x31 -> x17, waiting for transfers between devices: 48.5 us -> 25.4 us  [swap(): return lax.ppermute(x, axis, [(i, i ^ step) for i in range(n)])]
    pallas_call x6 -> x10, Pallas kernels: 32.3 us -> 9.44 us  [call(): pl.pallas_call(kernel, in_specs=specs or [VMEM] * len(args), out_specs=[V...]
    ppermute x31 -> x17, starting transfers between devices: 30.7 us -> 20.9 us  [swap(): return lax.ppermute(x, axis, [(i, i ^ step) for i in range(n)])]
    unnamed x62 -> x32, local copies, waits for them, and re-layouts: 4.55 us -> 1.59 us
    all_to_all x1, blocking collectives: 10.7 us -> 12.7 us  [shards(): lax.all_to_all(parts, ('feat', 'tok'), 0, 0, tiled=True).sum(axis=0)]
    reshape x1 -> x0, local copies, waits for them, and re-layouts: 1.32 us -> none  [shards(): token_index.reshape(-1, 1)]
  transfers between devices with their start and end apart: 31 -> 17, of which waited for: 15 -> 9; matrix products, arithmetic and copies ran while one was open for 0% -> 0% of each run, Pallas kernels for 22% -> 11%
where the time goes in v2:
time: 71.7 us; the launch traced here: 71.5 us
  waiting for transfers between devices  25.4 us (35%)
  starting transfers between devices  20.9 us (29%)
  blocking collectives  12.7 us (18%)
  Pallas kernels  9.44 us (13%)
  local copies, waits for them, and re-layouts  1.59 us (2%)
  between operations  0.88 us (1%)
    ppermute x17, waiting for transfers between devices, swap(): return lax.ppermute(x, axis, [(i, i ^ step) for i in range(n)])  25.4 us
    ppermute x17, starting transfers between devices, swap(): return lax.ppermute(x, axis, [(i, i ^ step) for i in range(n)])  20.9 us
    all_to_all x1, blocking collectives, shards(): lax.all_to_all(parts, ('feat', 'tok'), 0, 0, tiled=True).sum(axis=0)  12.7 us
    pallas_call x10, Pallas kernels, call(): pl.pallas_call(kernel, in_specs=specs or [VMEM] * len(args), out_specs=[V...  9.44 us
    unnamed x32, local copies, waits for them, and re-layouts  1.59 us
  transfers between devices with their start and end apart: 17, of which 9 were waited for; matrix products, arithmetic and copies ran while one was open for 0% of the time, Pallas kernels for 11%

profile of v2, /device:TPU:0, one launch (start us, length us, event | category | flops | bytes accessed | tf_op | source)
XLA Modules:
  0.0 71.5 jit_solution(4759957493229433984)
XLA Ops:
  0.7 0.9 %copy-done.2 = bf16[16,2048]{1,0:T(8,128)(2,1)S(1)} copy-done((bf16[16,2048]{1,0:T(8,128)(2,1)S(1)}, bf16[16,2048]{1,0:T(8,128)(2,1)}, u32[]{:S(2)}) %copy-start.2) | copy-done | bytes 65560
  1.5 0.7 copy-done.3
  2.2 0.3 shard_map.85.refs_0_
  2.5 3.1 %collective-permute-start = (bf16[16,2048]{1,0:T(8,128)(2,1)S(1)}, bf16[16,2048]{1,0:T(8,128)(2,1)S(1)}, u32[]{:S(2)}, u32[]{:S(2)}) collective-permute-start(bf16[16,2048]{1,0:T(8,128)(2,1)S(1)} %shard_map.85.refs_0_), channel_id=1, source_target_pairs={{0,4},{2,6},{4,0},{6,2},{8,12},{10,14},{12,8},{14,10},{1,5},{3,7},... | collective-permute-start | bytes 196616 | tf_op jit(solution)/shard_map/ppermute | solution.py:34
  5.6 2.6 %collective-permute-start.1 = (bf16[16,2048]{1,0:T(8,128)(2,1)S(1)}, bf16[16,2048]{1,0:T(8,128)(2,1)S(1)}, u32[]{:S(2)}, u32[]{:S(2)}) collective-permute-start(bf16[16,2048]{1,0:T(8,128)(2,1)S(1)} %shard_map.85.refs_0_), channel_id=1, source_target_pairs={{0,8},{2,10},{4,12},{6,14},{8,0},{10,2},{12,4},{14,6},{1,9},{3,11}... | collective-permute-start | bytes 196616 | tf_op jit(solution)/shard_map/ppermute | solution.py:34
  8.2 4.7 %collective-permute-done.1.refs_2_ = bf16[16,2048]{1,0:T(8,128)(2,1)S(1)} collective-permute-done((bf16[16,2048]{1,0:T(8,128)(2,1)S(1)}, bf16[16,2048]{1,0:T(8,128)(2,1)S(1)}, u32[]{:S(2)}, u32[]{:S(2)}) %collective-permute-start.1) | collective-permute-done | bytes 65568 | tf_op jit(solution)/shard_map/ppermute | solution.py:34
  12.8 1.4 %collective-permute-done.2.refs_3_ = bf16[16,2048]{1,0:T(8,128)(2,1)S(1)} collective-permute-done((bf16[16,2048]{1,0:T(8,128)(2,1)S(1)}, bf16[16,2048]{1,0:T(8,128)(2,1)S(1)}, u32[]{:S(2)}, u32[]{:S(2)}) %collective-permute-start.2) | collective-permute-done | bytes 65568 | tf_op jit(solution)/shard_map/ppermute | solution.py:34
  14.3 0.2 shard_map.86
  14.5 1.6 %collective-permute-start.3 = (bf16[4,16,2048]{2,1,0:T(8,128)(2,1)S(1)}, bf16[4,16,2048]{2,1,0:T(8,128)(2,1)S(1)}, u32[]{:S(2)}, u32[]{:S(2)}) collective-permute-start(bf16[4,16,2048]{2,1,0:T(8,128)(2,1)S(1)} %get-tuple-element.15), channel_id=1, source_target_pairs={{0,2},{2,0},{4,6},{6,4},{8,10},{10,8},{12,14},{14,12},{1,3},{3,1},... | collective-permute-start | bytes 786440 | tf_op jit(solution)/shard_map/ppermute | solution.py:34
  16.1 2.3 %collective-permute-start.9 = (bf16[16,7168]{1,0:T(8,128)(2,1)S(1)}, bf16[16,7168]{1,0:T(8,128)(2,1)S(1)}, u32[]{:S(2)}, u32[]{:S(2)}) collective-permute-start(bf16[16,7168]{1,0:T(8,128)(2,1)S(1)} %get-tuple-element.19.refs_0_), channel_id=1, source_target_pairs={{0,8},{2,10},{4,12},{6,14},{8,0},{10,2},{12,4},{14,6},{1,9},{3,11}... | collective-permute-start | bytes 688136 | tf_op jit(solution)/shard_map/ppermute | solution.py:34
  18.5 2.0 %collective-permute-start.10 = (bf16[16,7168]{1,0:T(8,128)(2,1)S(1)}, bf16[16,7168]{1,0:T(8,128)(2,1)S(1)}, u32[]{:S(2)}, u32[]{:S(2)}) collective-permute-start(bf16[16,7168]{1,0:T(8,128)(2,1)S(1)} %get-tuple-element.19.refs_0_), channel_id=1, source_target_pairs={{0,12},{2,14},{4,8},{6,10},{8,4},{10,6},{12,0},{14,2},{1,13},{3,15... | collective-permute-start | bytes 688136 | tf_op jit(solution)/shard_map/ppermute | solution.py:34
  20.5 0.5 collective-permute-done.3.refs_4_
  21.0 0.7 shard_map.87
  21.8 3.2 %collective-permute-done.8.refs_1_ = bf16[16,7168]{1,0:T(8,128)(2,1)S(1)} collective-permute-done((bf16[16,7168]{1,0:T(8,128)(2,1)S(1)}, bf16[16,7168]{1,0:T(8,128)(2,1)S(1)}, u32[]{:S(2)}, u32[]{:S(2)}) %collective-permute-start.8) | collective-permute-done | bytes 229408 | tf_op jit(solution)/shard_map/ppermute | solution.py:34
  25.1 0.6 collective-permute-start.11
  25.7 0.6 shard_map.88
  26.3 8.9 %collective-permute-done.9.refs_0_.refs_2_ = bf16[16,7168]{1,0:T(8,128)(2,1)S(1)} collective-permute-done((bf16[16,7168]{1,0:T(8,128)(2,1)S(1)}, bf16[16,7168]{1,0:T(8,128)(2,1)S(1)}, u32[]{:S(2)}, u32[]{:S(2)}) %collective-permute-start.9) | collective-permute-done | bytes 229408 | tf_op jit(solution)/shard_map/ppermute | solution.py:34
  35.2 0.6 collective-permute-start.12
  35.8 3.0 %collective-permute-start.5 = (bf16[128,256]{1,0:T(8,128)(2,1)S(1)}, bf16[128,256]{1,0:T(8,128)(2,1)S(1)}, u32[]{:S(2)}, u32[]{:S(2)}) collective-permute-start(bf16[128,256]{1,0:T(8,128)(2,1)S(1)} %get-tuple-element.18.refs_0_.refs_2_), channel_id=1, source_target_pairs={{0,4},{2,6},{4,0},{6,2},{8,12},{10,14},{12,8},{14,10},{1,5},{3,7},... | collective-permute-start | bytes 196616 | tf_op jit(solution)/shard_map/ppermute | solution.py:34
  38.8 1.3 %collective-permute-start.6 = (bf16[128,256]{1,0:T(8,128)(2,1)S(1)}, bf16[128,256]{1,0:T(8,128)(2,1)S(1)}, u32[]{:S(2)}, u32[]{:S(2)}) collective-permute-start(bf16[128,256]{1,0:T(8,128)(2,1)S(1)} %get-tuple-element.18.refs_0_.refs_2_), channel_id=1, source_target_pairs={{0,8},{2,10},{4,12},{6,14},{8,0},{10,2},{12,4},{14,6},{1,9},{3,11}... | collective-permute-start | bytes 196616 | tf_op jit(solution)/shard_map/ppermute | solution.py:34
  40.1 1.5 %collective-permute-start.7 = (bf16[128,256]{1,0:T(8,128)(2,1)S(1)}, bf16[128,256]{1,0:T(8,128)(2,1)S(1)}, u32[]{:S(2)}, u32[]{:S(2)}) collective-permute-start(bf16[128,256]{1,0:T(8,128)(2,1)S(1)} %get-tuple-element.18.refs_0_.refs_2_), channel_id=1, source_target_pairs={{0,12},{2,14},{4,8},{6,10},{8,4},{10,6},{12,0},{14,2},{1,13},{3,15... | collective-permute-start | bytes 196616 | tf_op jit(solution)/shard_map/ppermute | solution.py:34
  41.6 3.1 %collective-permute-done.6.refs_2_ = bf16[128,256]{1,0:T(8,128)(2,1)S(1)} collective-permute-done((bf16[128,256]{1,0:T(8,128)(2,1)S(1)}, bf16[128,256]{1,0:T(8,128)(2,1)S(1)}, u32[]{:S(2)}, u32[]{:S(2)}) %collective-permute-start.6) | collective-permute-done | bytes 65568 | tf_op jit(solution)/shard_map/ppermute | solution.py:34
  44.7 1.6 %collective-permute-done.7.refs_3_ = bf16[128,256]{1,0:T(8,128)(2,1)S(1)} collective-permute-done((bf16[128,256]{1,0:T(8,128)(2,1)S(1)}, bf16[128,256]{1,0:T(8,128)(2,1)S(1)}, u32[]{:S(2)}, u32[]{:S(2)}) %collective-permute-start.7) | collective-permute-done | bytes 65568 | tf_op jit(solution)/shard_map/ppermute | solution.py:34
  46.3 1.6 %collective-permute-start.14 = (bf16[4,128,256]{2,1,0:T(8,128)(2,1)S(1)}, bf16[4,128,256]{2,1,0:T(8,128)(2,1)S(1)}, u32[]{:S(2)}, u32[]{:S(2)}) collective-permute-start(bf16[4,128,256]{2,1,0:T(8,128)(2,1)S(1)} %shard_map.89.refs_0_), channel_id=1, source_target_pairs={{0,2},{2,0},{4,6},{6,4},{8,10},{10,8},{12,14},{14,12},{1,3},{3,1},... | collective-permute-start | bytes 786440 | tf_op jit(solution)/shard_map/ppermute | solution.py:34
  48.0 4.3 %shard_map.92 = (f32[128,896]{1,0:T(8,128)S(1)}, f32[128,896]{1,0:T(8,128)S(1)}) custom-call(bf16[16,7168]{1,0:T(8,128)(2,1)S(1)} %get-tuple-element.19.refs_0_, bf16[16,7168]{1,0:T(8,128)(2,1)S(1)} %collective-permute-done.8.refs_1_, bf16[16,7168]{1,0:T(8,128)(2,1)S(1)} %collective-permute-done.9.refs_0_.refs_2_, ...), custom_call_target="tpu_custom_call" | custom-call | flops 11744051200 | bytes 25690112 | tf_op jit(solution)/shard_map/pallas_call | solution.py:21
  52.4 0.5 collective-permute-start.15
  53.0 1.6 %collective-permute-done.15.refs_2_ = bf16[4,128,256]{2,1,0:T(8,128)(2,1)S(1)} collective-permute-done((bf16[4,128,256]{2,1,0:T(8,128)(2,1)S(1)}, bf16[4,128,256]{2,1,0:T(8,128)(2,1)S(1)}, u32[]{:S(2)}, u32[]{:S(2)}) %collective-permute-start.15) | collective-permute-done | bytes 262176 | tf_op jit(solution)/shard_map/ppermute | solution.py:34
  54.6 0.4 collective-permute-done.16.refs_3_
  55.0 2.4 %shard_map.93.wide = f32[2,128,896]{2,1,0:T(8,128)S(1)} custom-call(bf16[4,128,256]{2,1,0:T(8,128)(2,1)S(1)} %shard_map.89.refs_0_, bf16[4,128,256]{2,1,0:T(8,128)(2,1)S(1)} %collective-permute-done.14.refs_1_, bf16[4,128,256]{2,1,0:T(8,128)(2,1)S(1)} %collective-permute-done.15.refs_2_, bf16[4,128,256]{2,1,0:T(8,128)(2,1)S(1)} %collective-permute-done.16.refs_3_, ...), custom_call_target="tpu_custom_call" | custom-call | flops 1879048192 | bytes 14680064 | tf_op jit(solution)/shard_map/pallas_call | solution.py:21
  57.4 0.8 %shard_map.94 = (bf16[128,896]{1,0:T(8,128)(2,1)}, f32[16,2,128]{2,1,0:T(2,128)S(1)}) custom-call(f32[128,896]{1,0:T(8,128)S(1)} %get-tuple-element.20.mine, f32[128,896]{1,0:T(8,128)S(1)} %collective-permute-done.13.theirs, f32[2,128,896]{2,1,0:T(8,128)S(1)} %shard_map.93.wide), custom_call_target="tpu_custom_call" | custom-call | tf_op jit(solution)/shard_map/pallas_call | solution.py:21
  58.2 12.7 %all_to_all.5 = f32[16,2,128]{2,1,0:T(2,128)S(1)} all-to-all(f32[16,2,128]{2,1,0:T(2,128)S(1)} %get-tuple-element.22), channel_id=1, replica_groups=mesh['parts'=2,'feat'=8,'tok'=2] {'feat','tok'}, dimensions={0} | all-to-all | bytes 32768 | tf_op jit(solution)/shard_map/all_to_all | solution.py:189
  70.9 0.6 reduce_sum.9
  (48 shorter events, 0.4 us)
Async XLA Ops:
  0.6 13.6 %copy-start.1 = (bf16[16,7168]{1,0:T(8,128)(2,1)S(1)}, bf16[16,7168]{1,0:T(8,128)(2,1)}, u32[]{:S(2)}) copy-start(bf16[16,7168]{1,0:T(8,128)(2,1)} %pool.3) | copy-start | bytes 688132
  0.6 0.9 %copy-start.2 = (bf16[16,2048]{1,0:T(8,128)(2,1)S(1)}, bf16[16,2048]{1,0:T(8,128)(2,1)}, u32[]{:S(2)}) copy-start(bf16[16,2048]{1,0:T(8,128)(2,1)} %pool.2) | copy-start | bytes 196612
  2.2 12.1 %copy-start.4 = (s32[1,16]{1,0:T(1,128)S(1)}, s32[1,16]{1,0:T(1,128)}, u32[]{:S(2)}) copy-start(s32[1,16]{1,0:T(1,128)} %order_ref.3) | copy-start | bytes 196
  2.5 18.6 %copy-start = (bf16[2048,512]{1,0:T(8,128)(2,1)S(1)}, bf16[2048,512]{1,0:T(8,128)(2,1)}, u32[]{:S(2)}) copy-start(bf16[2048,512]{1,0:T(8,128)(2,1)} %refs_5_.1) | copy-start | bytes 6291460
  2.5 5.7 %collective-permute-start = (bf16[16,2048]{1,0:T(8,128)(2,1)S(1)}, bf16[16,2048]{1,0:T(8,128)(2,1)S(1)}, u32[]{:S(2)}, u32[]{:S(2)}) collective-permute-start(bf16[16,2048]{1,0:T(8,128)(2,1)S(1)} %shard_map.85.refs_0_), channel_id=1, source_target_pairs={{0,4},{2,6},{4,0},{6,2},{8,12},{10,14},{12,8},{14,10},{1,5},{3,7},... | collective-permute-start | bytes 196616 | tf_op jit(solution)/shard_map/ppermute | solution.py:34
  5.6 7.3 %collective-permute-start.1 = (bf16[16,2048]{1,0:T(8,128)(2,1)S(1)}, bf16[16,2048]{1,0:T(8,128)(2,1)S(1)}, u32[]{:S(2)}, u32[]{:S(2)}) collective-permute-start(bf16[16,2048]{1,0:T(8,128)(2,1)S(1)} %shard_map.85.refs_0_), channel_id=1, source_target_pairs={{0,8},{2,10},{4,12},{6,14},{8,0},{10,2},{12,4},{14,6},{1,9},{3,11}... | collective-permute-start | bytes 196616 | tf_op jit(solution)/shard_map/ppermute | solution.py:34
  8.2 6.1 %collective-permute-start.2 = (bf16[16,2048]{1,0:T(8,128)(2,1)S(1)}, bf16[16,2048]{1,0:T(8,128)(2,1)S(1)}, u32[]{:S(2)}, u32[]{:S(2)}) collective-permute-start(bf16[16,2048]{1,0:T(8,128)(2,1)S(1)} %shard_map.85.refs_0_), channel_id=1, source_target_pairs={{0,12},{2,14},{4,8},{6,10},{8,4},{10,6},{12,0},{14,2},{1,13},{3,15... | collective-permute-start | bytes 196616 | tf_op jit(solution)/shard_map/ppermute | solution.py:34
  14.2 33.7 %slice-start.4 = ((s8[25690112]{0:T(1024)(128)(4,1)}), s8[4194304]{0:T(1024)(128)(4,1)S(1)}, s32[]{:S(2)}) async-start(s8[25690112]{0:T(1024)(128)(4,1)} %bitcast.2), calls=%async_computation.5 | async-start | bytes 8388608
  14.2 33.7 %slice-start.5 = ((s8[25690112]{0:T(1024)(128)(4,1)}), s8[4194304]{0:T(1024)(128)(4,1)S(1)}, s32[]{:S(2)}) async-start(s8[25690112]{0:T(1024)(128)(4,1)} %bitcast.2), calls=%async_computation.6 | async-start | bytes 8388608
  14.2 33.7 %slice-start.6 = ((s8[25690112]{0:T(1024)(128)(4,1)}), s8[4194304]{0:T(1024)(128)(4,1)S(1)}, s32[]{:S(2)}) async-start(s8[25690112]{0:T(1024)(128)(4,1)} %bitcast.2), calls=%async_computation.7 | async-start | bytes 8388608
  14.3 33.7 %slice-start.7 = ((s8[25690112]{0:T(1024)(128)(4,1)}), s8[4194304]{0:T(1024)(128)(4,1)S(1)}, s32[]{:S(2)}) async-start(s8[25690112]{0:T(1024)(128)(4,1)} %bitcast.2), calls=%async_computation.8 | async-start | bytes 8388608
  14.3 33.7 %slice-start.8 = ((s8[25690112]{0:T(1024)(128)(4,1)}), s8[4194304]{0:T(1024)(128)(4,1)S(1)}, s32[]{:S(2)}) async-start(s8[25690112]{0:T(1024)(128)(4,1)} %bitcast.2), calls=%async_computation.9 | async-start | bytes 8388608
  14.5 6.5 %collective-permute-start.3 = (bf16[4,16,2048]{2,1,0:T(8,128)(2,1)S(1)}, bf16[4,16,2048]{2,1,0:T(8,128)(2,1)S(1)}, u32[]{:S(2)}, u32[]{:S(2)}) collective-permute-start(bf16[4,16,2048]{2,1,0:T(8,128)(2,1)S(1)} %get-tuple-element.15), channel_id=1, source_target_pairs={{0,2},{2,0},{4,6},{6,4},{8,10},{10,8},{12,14},{14,12},{1,3},{3,1},... | collective-permute-start | bytes 786440 | tf_op jit(solution)/shard_map/ppermute | solution.py:34
  16.1 31.9 %slice-start.9 = ((s8[25690112]{0:T(1024)(128)(4,1)}), s8[4194304]{0:T(1024)(128)(4,1)S(1)}, s32[]{:S(2)}) async-start(s8[25690112]{0:T(1024)(128)(4,1)} %bitcast.2), calls=%async_computation.10 | async-start | bytes 8388608
  16.1 31.9 %slice-start.10 = ((s8[25690112]{0:T(1024)(128)(4,1)}), s8[524288]{0:T(1024)(128)(4,1)S(1)}, s32[]{:S(2)}) async-start(s8[25690112]{0:T(1024)(128)(4,1)} %bitcast.2), calls=%async_computation.11 | async-start | bytes 1048576
  16.1 8.9 %collective-permute-start.8 = (bf16[16,7168]{1,0:T(8,128)(2,1)S(1)}, bf16[16,7168]{1,0:T(8,128)(2,1)S(1)}, u32[]{:S(2)}, u32[]{:S(2)}) collective-permute-start(bf16[16,7168]{1,0:T(8,128)(2,1)S(1)} %get-tuple-element.19.refs_0_), channel_id=1, source_target_pairs={{0,4},{2,6},{4,0},{6,2},{8,12},{10,14},{12,8},{14,10},{1,5},{3,7},... | collective-permute-start | bytes 688136 | tf_op jit(solution)/shard_map/ppermute | solution.py:34
  16.1 19.1 %collective-permute-start.9 = (bf16[16,7168]{1,0:T(8,128)(2,1)S(1)}, bf16[16,7168]{1,0:T(8,128)(2,1)S(1)}, u32[]{:S(2)}, u32[]{:S(2)}) collective-permute-start(bf16[16,7168]{1,0:T(8,128)(2,1)S(1)} %get-tuple-element.19.refs_0_), channel_id=1, source_target_pairs={{0,8},{2,10},{4,12},{6,14},{8,0},{10,2},{12,4},{14,6},{1,9},{3,11}... | collective-permute-start | bytes 688136 | tf_op jit(solution)/shard_map/ppermute | solution.py:34
  18.5 16.7 %collective-permute-start.10 = (bf16[16,7168]{1,0:T(8,128)(2,1)S(1)}, bf16[16,7168]{1,0:T(8,128)(2,1)S(1)}, u32[]{:S(2)}, u32[]{:S(2)}) collective-permute-start(bf16[16,7168]{1,0:T(8,128)(2,1)S(1)} %get-tuple-element.19.refs_0_), channel_id=1, source_target_pairs={{0,12},{2,14},{4,8},{6,10},{8,4},{10,6},{12,0},{14,2},{1,13},{3,15... | collective-permute-start | bytes 688136 | tf_op jit(solution)/shard_map/ppermute | solution.py:34
  21.7 3.9 %collective-permute-start.4 = (f32[128,256]{1,0:T(8,128)S(1)}, f32[128,256]{1,0:T(8,128)S(1)}, u32[]{:S(2)}, u32[]{:S(2)}) collective-permute-start(f32[128,256]{1,0:T(8,128)S(1)} %get-tuple-element.17), channel_id=1, source_target_pairs={{0,1},{1,0},{2,3},{3,2},{4,5},{5,4},{6,7},{7,6},{8,9},{9,8},{10,11... | collective-permute-start | bytes 393224 | tf_op jit(solution)/shard_map/ppermute | solution.py:34
  25.1 22.8 %collective-permute-start.11 = (bf16[2,16,7168]{2,1,0:T(8,128)(2,1)S(1)}, bf16[2,16,7168]{2,1,0:T(8,128)(2,1)S(1)}, u32[]{:S(2)}, u32[]{:S(2)}) collective-permute-start(bf16[2,16,7168]{2,1,0:T(8,128)(2,1)S(1)} %shard_map.90), channel_id=1, source_target_pairs={{0,2},{2,0},{4,6},{6,4},{8,10},{10,8},{12,14},{14,12},{1,3},{3,1},... | collective-permute-start | bytes 1376264 | tf_op jit(solution)/shard_map/ppermute | solution.py:34
  35.2 12.7 %collective-permute-start.12 = (bf16[2,16,7168]{2,1,0:T(8,128)(2,1)S(1)}, bf16[2,16,7168]{2,1,0:T(8,128)(2,1)S(1)}, u32[]{:S(2)}, u32[]{:S(2)}) collective-permute-start(bf16[2,16,7168]{2,1,0:T(8,128)(2,1)S(1)} %shard_map.91), channel_id=1, source_target_pairs={{0,2},{2,0},{4,6},{6,4},{8,10},{10,8},{12,14},{14,12},{1,3},{3,1},... | collective-permute-start | bytes 1376264 | tf_op jit(solution)/shard_map/ppermute | solution.py:34
  35.8 5.8 %collective-permute-start.5 = (bf16[128,256]{1,0:T(8,128)(2,1)S(1)}, bf16[128,256]{1,0:T(8,128)(2,1)S(1)}, u32[]{:S(2)}, u32[]{:S(2)}) collective-permute-start(bf16[128,256]{1,0:T(8,128)(2,1)S(1)} %get-tuple-element.18.refs_0_.refs_2_), channel_id=1, source_target_pairs={{0,4},{2,6},{4,0},{6,2},{8,12},{10,14},{12,8},{14,10},{1,5},{3,7},... | collective-permute-start | bytes 196616 | tf_op jit(solution)/shard_map/ppermute | solution.py:34
  38.8 5.9 %collective-permute-start.6 = (bf16[128,256]{1,0:T(8,128)(2,1)S(1)}, bf16[128,256]{1,0:T(8,128)(2,1)S(1)}, u32[]{:S(2)}, u32[]{:S(2)}) collective-permute-start(bf16[128,256]{1,0:T(8,128)(2,1)S(1)} %get-tuple-element.18.refs_0_.refs_2_), channel_id=1, source_target_pairs={{0,8},{2,10},{4,12},{6,14},{8,0},{10,2},{12,4},{14,6},{1,9},{3,11}... | collective-permute-start | bytes 196616 | tf_op jit(solution)/shard_map/ppermute | solution.py:34
  40.1 6.2 %collective-permute-start.7 = (bf16[128,256]{1,0:T(8,128)(2,1)S(1)}, bf16[128,256]{1,0:T(8,128)(2,1)S(1)}, u32[]{:S(2)}, u32[]{:S(2)}) collective-permute-start(bf16[128,256]{1,0:T(8,128)(2,1)S(1)} %get-tuple-element.18.refs_0_.refs_2_), channel_id=1, source_target_pairs={{0,12},{2,14},{4,8},{6,10},{8,4},{10,6},{12,0},{14,2},{1,13},{3,15... | collective-permute-start | bytes 196616 | tf_op jit(solution)/shard_map/ppermute | solution.py:34
  46.3 8.7 %slice-start = ((s8[14680064]{0:T(1024)(128)(4,1)}), s8[4194304]{0:T(1024)(128)(4,1)S(1)}, s32[]{:S(2)}) async-start(s8[14680064]{0:T(1024)(128)(4,1)} %bitcast), calls=%async_computation.1 | async-start | bytes 8388608
  46.3 8.7 %slice-start.1 = ((s8[14680064]{0:T(1024)(128)(4,1)}), s8[4194304]{0:T(1024)(128)(4,1)S(1)}, s32[]{:S(2)}) async-start(s8[14680064]{0:T(1024)(128)(4,1)} %bitcast), calls=%async_computation.2 | async-start | bytes 8388608
  46.3 8.7 %slice-start.2 = ((s8[14680064]{0:T(1024)(128)(4,1)}), s8[4194304]{0:T(1024)(128)(4,1)S(1)}, s32[]{:S(2)}) async-start(s8[14680064]{0:T(1024)(128)(4,1)} %bitcast), calls=%async_computation.3 | async-start | bytes 8388608
  46.3 8.7 %slice-start.3 = ((s8[14680064]{0:T(1024)(128)(4,1)}), s8[2097152]{0:T(1024)(128)(4,1)S(1)}, s32[]{:S(2)}) async-start(s8[14680064]{0:T(1024)(128)(4,1)} %bitcast), calls=%async_computation.4 | async-start | bytes 4194304
  46.3 6.6 %collective-permute-start.14 = (bf16[4,128,256]{2,1,0:T(8,128)(2,1)S(1)}, bf16[4,128,256]{2,1,0:T(8,128)(2,1)S(1)}, u32[]{:S(2)}, u32[]{:S(2)}) collective-permute-start(bf16[4,128,256]{2,1,0:T(8,128)(2,1)S(1)} %shard_map.89.refs_0_), channel_id=1, source_target_pairs={{0,2},{2,0},{4,6},{6,4},{8,10},{10,8},{12,14},{14,12},{1,3},{3,1},... | collective-permute-start | bytes 786440 | tf_op jit(solution)/shard_map/ppermute | solution.py:34
  52.4 5.0 %collective-permute-start.13 = (f32[128,896]{1,0:T(8,128)S(1)}, f32[128,896]{1,0:T(8,128)S(1)}, u32[]{:S(2)}, u32[]{:S(2)}) collective-permute-start(f32[128,896]{1,0:T(8,128)S(1)} %get-tuple-element.21), channel_id=1, source_target_pairs={{0,1},{1,0},{2,3},{3,2},{4,5},{5,4},{6,7},{7,6},{8,9},{9,8},{10,11... | collective-permute-start | bytes 1376264 | tf_op jit(solution)/shard_map/ppermute | solution.py:34
  52.4 2.2 %collective-permute-start.15 = (bf16[4,128,256]{2,1,0:T(8,128)(2,1)S(1)}, bf16[4,128,256]{2,1,0:T(8,128)(2,1)S(1)}, u32[]{:S(2)}, u32[]{:S(2)}) collective-permute-start(bf16[4,128,256]{2,1,0:T(8,128)(2,1)S(1)} %shard_map.89.refs_0_), channel_id=1, source_target_pairs={{0,1},{1,0},{2,3},{3,2},{4,5},{5,4},{6,7},{7,6},{8,9},{9,8},{10,11... | collective-permute-start | bytes 786440 | tf_op jit(solution)/shard_map/ppermute | solution.py:34
  52.9 2.1 %collective-permute-start.16 = (bf16[4,128,256]{2,1,0:T(8,128)(2,1)S(1)}, bf16[4,128,256]{2,1,0:T(8,128)(2,1)S(1)}, u32[]{:S(2)}, u32[]{:S(2)}) collective-permute-start(bf16[4,128,256]{2,1,0:T(8,128)(2,1)S(1)} %collective-permute-done.14.refs_1_), channel_id=1, source_target_pairs={{0,1},{1,0},{2,3},{3,2},{4,5},{5,4},{6,7},{7,6},{8,9},{9,8},{10,11... | collective-permute-start | bytes 786440 | tf_op jit(solution)/shard_map/ppermute | solution.py:34
  (1 other events, 0.7 us)

commit v3 on v2

v3 whole, which is shorter than its diff:
```python
import functools
import math

import jax
import jax.numpy as jnp
from jax import lax
from jax.experimental import pallas as pl
from jax.experimental.pallas import tpu as pltpu
from jax.sharding import PartitionSpec as P

BF16 = jnp.bfloat16
F32 = jnp.float32
VMEM = pl.BlockSpec(memory_space=pltpu.VMEM)
ANY = pl.BlockSpec(memory_space=pl.ANY)
ROOM = 4 * 2**20


def call(kernel, outs, *args, scratch=(), flops=0, read=0, specs=None, room=ROOM):
    held = [(s.shape, s.dtype) for s in scratch if getattr(s, "memory_space", None) == pltpu.VMEM] + list(outs)
    held = sum(math.prod(shape) * jnp.dtype(dtype).itemsize for shape, dtype in held)
    return pl.pallas_call(
        kernel,
        in_specs=specs or [VMEM] * len(args),
        out_specs=[VMEM] * len(outs),
        out_shape=[jax.ShapeDtypeStruct(*o) for o in outs],
        scratch_shapes=list(scratch),
        compiler_params=pltpu.CompilerParams(vmem_limit_bytes=room + held),
        cost_estimate=pl.CostEstimate(flops=flops, bytes_accessed=read, transcendentals=0),
    )(*args)


def swap(x, axis, step):
    n = lax.axis_size(axis)
    return lax.ppermute(x, axis, [(i, i ^ step) for i in range(n)])


def pick(order_ref, pool):
    n = pool.shape[0]
    hot = (order_ref[...] == lax.broadcasted_iota(jnp.int32, (n, n), 0)).astype(BF16)
    rows = lax.dot_general(hot, pool[...], (((0,), (0,)), ((), ())), preferred_element_type=F32)
    return rows.astype(BF16)


def select(token_index, pool, deps=(), flops=0):
    hot = (token_index[0][:, None] == jnp.arange(pool.shape[0])[None]).astype(BF16)
    if deps:
        hot = after(hot, *deps)
    return jnp.dot(hot, pool, preferred_element_type=F32).astype(BF16)


def halves(total, keep, give):
    half = total.shape[1] // 2
    low, high = total[:, :half], total[:, half:]
    first = lax.axis_index("tok") == 0
    keep[...] = jnp.where(first, low, high)
    give[...] = jnp.where(first, high, low)


def bundle_kernel(count, *refs):
    out = refs[-1]
    for i in range(count):
        out[i] = refs[i][...]


def bundle(xs, deps=(), flops=0):
    (out,) = call(
        functools.partial(bundle_kernel, len(xs)), [((len(xs),) + xs[0].shape, xs[0].dtype)],
        *xs, *deps, specs=[VMEM] * len(xs) + [ANY] * len(deps), flops=flops,
    )
    return out


def is_inner(me):
    z = me // 2
    return ((z ^ (z // 2)) & 1) == 1


def choose_kernel(inner_ref, end_ref, out):
    out[...] = jnp.where(is_inner(lax.axis_index("feat")), inner_ref[...], end_ref[...])


def choose(inner, end):
    return call(choose_kernel, [(inner.shape, inner.dtype)], inner, end)[0]


def pair_middle(x):
    to = [i ^ 6 if i // 2 in (1, 2) else i ^ 1 for i in range(8)]
    return lax.ppermute(x, "feat", list(enumerate(to)))


def relay_place(me):
    z, y = me // 2, me % 2
    inner = is_inner(me)
    mid = jnp.where(inner, z ^ 3, z ^ 2)
    near, other = z ^ 1, y ^ 1
    out = mid ^ 1
    return [
        z * 2 + y,
        near * 2 + y,
        jnp.where(inner, mid * 2 + y, z * 2 + other),
        jnp.where(inner, out * 2 + y, near * 2 + other),
        jnp.where(inner, near * 2 + other, mid * 2 + y),
        jnp.where(inner, z * 2 + other, out * 2 + y),
        mid * 2 + other,
        out * 2 + other,
    ]


def direct_place(me, m):
    return [me ^ (2 * i + side) for side in range(2) for i in range(m)]


def rows_of(refs):
    return [ref.at[i] for ref in refs for i in range(ref.shape[0])]


def rotate_kernel(depth, place, *refs):
    shards = rows_of(refs[:-5])
    basis, keep, give, rows, total = refs[-5:]
    n = shards[0].shape[0]
    for owner, shard in zip(place(lax.axis_index("feat")), shards):
        rows[pl.ds(pl.multiple_of(owner * n, n), n), :] = shard[...]
    total[...] = jnp.zeros_like(total)

    def body(i, carry):
        at = pl.ds(pl.multiple_of(i * depth, depth), depth)
        total[...] += jnp.dot(rows[:, at], basis[at, :], preferred_element_type=F32)
        return carry

    lax.fori_loop(0, basis.shape[0] // depth, body, 0)
    halves(total, keep, give)


def rotate(shards, place, basis, depth, flops):
    _, n, k = shards[0].shape
    tokens, width = n * lax.axis_size("feat"), basis.shape[1]
    half = ((tokens, width // 2), F32)
    return call(
        functools.partial(rotate_kernel, depth, place), [half, half], *shards, basis,
        scratch=[pltpu.VMEM((tokens, k), BF16), pltpu.VMEM((tokens, width), F32)],
        flops=flops, read=k * width * 2,
    )


def add_kernel(a_ref, b_ref, out, again):
    total = (a_ref[...] + b_ref[...]).astype(BF16)
    out[...] = total
    again[...] = total


def query_kernel(side, mine, theirs, precond, *refs):
    *so_far, out = refs
    me, tok = lax.axis_index("feat"), lax.axis_index("tok")
    count, _, w = mine.shape
    for q in range(precond.shape[0]):
        total = so_far[0][q] if so_far else None
        for i, block in enumerate((mine, theirs)):
            for j in range(count):
                owner = ((me ^ (2 * j + side)) * 2 + (tok ^ i)) * w
                part = precond[q, pl.ds(pl.multiple_of(owner, w), w), :]
                term = jnp.dot(block[j], part, preferred_element_type=F32)
                total = term if total is None else total + term
        out[q] = total


def query(side, mine, theirs, precond, so_far):
    queries, _, width = precond.shape
    tokens = mine.shape[1]
    (out,) = call(
        functools.partial(query_kernel, side), [((queries, tokens, width), F32)],
        mine, theirs, precond, *so_far,
        flops=tokens * precond.size, read=precond.size,
    )
    return out


def score_kernel(mine, theirs, wide, act_rot, out):
    rot = (mine[...] + theirs[...]).astype(BF16)
    act_rot[...] = rot
    rot = rot.astype(F32)
    value = jnp.sum(wide[...] * rot[None], axis=2)
    for i in range(out.shape[0]):
        out[i] = value


def across(x):
    return [x] + [swap(x, "feat", step) for step in range(2, lax.axis_size("feat"), 2)]


def after(x, *deps):
    return lax.optimization_barrier((x,) + deps)[0]


def shards(token_index, act_pool, grad_pool, basis_in, basis_out, precond):
    n = lax.axis_size("feat")
    stored, act_width = act_pool.shape
    tokens, queries = stored * n, precond.shape[0]
    m = n // 2
    relay = n == 8
    direct = functools.partial(direct_place, m=m)
    grads = select(token_index, grad_pool, flops=4000 * basis_out.size)
    near = across(grads)
    act = select(token_index, act_pool, near[1:2])
    first = [swap(act, "feat", 2), pair_middle(act)] if relay else [swap(act, "feat", 1)]
    near_bundle = bundle(near, [act], 800 * basis_in.size)
    far_bundle = after(swap(near_bundle, "feat", 1), *first)
    if relay:
        z1, m1 = first
        m2, o2 = pair_middle(z1), swap(m1, "feat", 2)
    else:
        act_near = across(after(act, near_bundle))
    keep, give = rotate(
        [near_bundle, far_bundle], direct, basis_out, basis_out.shape[0] // 2, 256 * basis_out.size,
    )
    grad_rot, block = call(
        add_kernel, [(keep.shape, BF16)] * 2, keep, swap(give, "tok", 1),
    )
    if relay:
        o3, y2 = swap(after(m2, block), "feat", 2), swap(choose(after(m1, block), o2), "feat", 1)
        mine = bundle(across(block), [o3, y2])
        y3 = swap(choose(m2, o3), "feat", 1)
        act_all, place = [act, z1, m1, m2, o2, o3, y2, y3], relay_place
    else:
        act_far = swap(bundle(act_near[1:], [block]), "feat", 1)
        mine = bundle(across(block))
        act_all, place = act_near + first + [act_far], direct
    wide = query(0, mine, swap(mine, "tok", 1), precond, [])
    other = swap(mine, "feat", 1)
    act_all[0] = after(act_all[0], wide)
    wide = query(1, other, swap(other, "tok", 1), precond, [wide])
    act_all = [x if x.ndim == 3 else x[None] for x in act_all]
    keep, give = rotate(act_all, place, basis_in, act_width // 4, 1600 * precond.size)
    act_rot, parts = call(
        score_kernel, [(keep.shape, BF16), ((2 * n, queries, tokens), F32)],
        keep, swap(give, "tok", 1), wide,
    )
    scores = lax.all_to_all(parts, ("feat", "tok"), 0, 0, tiled=True).sum(axis=0)
    return scores, act_rot, grad_rot


def solution(mesh):
    placed = (
        P(("parts", "feat"), None),
        P(("parts", "feat"), "tok"),
        P(("parts", "feat"), "tok"),
        P(("parts", "tok"), "feat"),
        P(("parts", "tok"), "feat"),
        P("parts", None, ("feat", "tok")),
    )
    return jax.shard_map(
        shards,
        mesh=mesh,
        in_specs=placed,
        out_specs=(P("parts", None), P("parts", ("feat", "tok")), P("parts", ("feat", "tok"))),
        check_vma=False,
    )
```

time: 71.7 us -> 68.1 us (0.950)
  blocking collectives: 12.7 us -> 10.3 us
  local copies, waits for them, and re-layouts: 1.59 us -> 0.04 us
  waiting for transfers between devices: 25.4 us -> 24 us
  matrix products: 0 us -> 1.29 us
  other arithmetic: 0.59 us -> 1.31 us
    ppermute x0 -> x2, starting transfers between devices: none -> 3.04 us  [pair_middle(): return lax.ppermute(x, 'feat', list(enumerate(to)))]
    ppermute x17, starting transfers between devices: 20.9 us -> 18 us  [swap(): return lax.ppermute(x, axis, [(i, i ^ step) for i in range(n)])]
    all_to_all x1, blocking collectives: 12.7 us -> 10.3 us  [shards(): lax.all_to_all(parts, ('feat', 'tok'), 0, 0, tiled=True).sum(axis=0)]
    unnamed x32 -> x14, local copies, waits for them, and re-layouts: 1.59 us -> 0.04 us
    ppermute x17, waiting for transfers between devices: 25.4 us -> 23.9 us  [swap(): return lax.ppermute(x, axis, [(i, i ^ step) for i in range(n)])]
    dot_general x0 -> x2, matrix products: none -> 1.29 us  [select(): return jnp.dot(hot, pool, preferred_element_type=F32).astype(BF16)]
    convert_element_type x0 -> x1, other arithmetic: none -> 0.73 us  [select(): (token_index[0][:, None] == jnp.arange(pool.shape[0])[None]).astype(BF16)]
  transfers between devices with their start and end apart: 17 -> 19, of which waited for: 9 -> 11; matrix products, arithmetic and copies ran while one was open for 0% -> 1% of each run, Pallas kernels for 11% -> 12%
where the time goes in v3:
time: 68.1 us; the launch traced here: 67.9 us
  waiting for transfers between devices  24 us (35%)
  starting transfers between devices  21 us (31%)
  blocking collectives  10.3 us (15%)
  Pallas kernels  9.13 us (13%)
  other arithmetic  1.31 us (2%)
  matrix products  1.29 us (2%)
  between operations  0.83 us (1%)
    ppermute x17, waiting for transfers between devices, swap(): return lax.ppermute(x, axis, [(i, i ^ step) for i in range(n)])  23.9 us
    ppermute x17, starting transfers between devices, swap(): return lax.ppermute(x, axis, [(i, i ^ step) for i in range(n)])  18 us
    all_to_all x1, blocking collectives, shards(): lax.all_to_all(parts, ('feat', 'tok'), 0, 0, tiled=True).sum(axis=0)  10.3 us
    pallas_call x10, Pallas kernels, call(): pl.pallas_call(kernel, in_specs=specs or [VMEM] * len(args), out_specs=[V...  9.13 us
    ppermute x2, starting transfers between devices, pair_middle(): return lax.ppermute(x, 'feat', list(enumerate(to)))  3.04 us
  transfers between devices with their start and end apart: 19, of which 11 were waited for; matrix products, arithmetic and copies ran while one was open for 1% of the time, Pallas kernels for 12%

profile of v3, /device:TPU:0, one launch (start us, length us, event | category | flops | bytes accessed | tf_op | source)
XLA Modules:
  0.0 67.9 jit_solution(9879734889269878575)
XLA Ops:
  0.6 1.1 %convolution_convert_fusion.1.refs_0_ = bf16[16,2048]{1,0:T(8,128)(2,1)S(1)} fusion(bf16[16,2048]{1,0:T(8,128)(2,1)} %param.8, s32[16]{0:T(128)} %bitcast.22), kind=kOutput, calls=%fused_computation.1 | convolution fusion | flops 1081600 | bytes 131136 | tf_op jit(solution)/shard_map/dot_general | solution.py:48
  1.7 3.1 %collective-permute-start = (bf16[16,2048]{1,0:T(8,128)(2,1)S(1)}, bf16[16,2048]{1,0:T(8,128)(2,1)S(1)}, u32[]{:S(2)}, u32[]{:S(2)}) collective-permute-start(bf16[16,2048]{1,0:T(8,128)(2,1)S(1)} %convolution_convert_fusion.1.refs_0_), channel_id=1, source_target_pairs={{0,4},{2,6},{4,0},{6,2},{8,12},{10,14},{12,8},{14,10},{1,5},{3,7},... | collective-permute-start | bytes 196616 | tf_op jit(solution)/shard_map/ppermute | solution.py:34
  4.8 2.6 %collective-permute-start.1 = (bf16[16,2048]{1,0:T(8,128)(2,1)S(1)}, bf16[16,2048]{1,0:T(8,128)(2,1)S(1)}, u32[]{:S(2)}, u32[]{:S(2)}) collective-permute-start(bf16[16,2048]{1,0:T(8,128)(2,1)S(1)} %convolution_convert_fusion.1.refs_0_), channel_id=1, source_target_pairs={{0,8},{2,10},{4,12},{6,14},{8,0},{10,2},{12,4},{14,6},{1,9},{3,11}... | collective-permute-start | bytes 196616 | tf_op jit(solution)/shard_map/ppermute | solution.py:34
  7.4 0.7 %fusion = bf16[16,16]{1,0:T(8,128)(2,1)S(1)} fusion(s32[16]{0:T(128)} %bitcast.23), kind=kLoop, calls=%fused_computation.3 | loop fusion | flops 512 | bytes 576 | tf_op jit(solution)/shard_map/convert_element_type | solution.py:45
  8.4 1.0 %collective-permute-start.4 = (bf16[16,7168]{1,0:T(8,128)(2,1)S(1)}, bf16[16,7168]{1,0:T(8,128)(2,1)S(1)}, u32[]{:S(2)}, u32[]{:S(2)}) collective-permute-start(bf16[16,7168]{1,0:T(8,128)(2,1)S(1)} %convolution_convert_fusion.refs_4_), channel_id=1, source_target_pairs={{0,4},{2,6},{4,0},{6,2},{8,12},{10,14},{12,8},{14,10},{1,5},{3,7},... | collective-permute-start | bytes 688136 | tf_op jit(solution)/shard_map/ppermute | solution.py:34
  9.4 1.5 %collective-permute-start.5 = (bf16[16,7168]{1,0:T(8,128)(2,1)S(1)}, bf16[16,7168]{1,0:T(8,128)(2,1)S(1)}, u32[]{:S(2)}, u32[]{:S(2)}) collective-permute-start(bf16[16,7168]{1,0:T(8,128)(2,1)S(1)} %convolution_convert_fusion.refs_4_), channel_id=1, source_target_pairs={{0,2},{2,0},{4,8},{6,10},{8,4},{10,6},{12,14},{14,12},{1,3},{3,1},... | collective-permute-start | bytes 688136 | tf_op jit(solution)/shard_map/ppermute | solution.py:88
  10.9 1.2 %collective-permute-done.1.refs_2_ = bf16[16,2048]{1,0:T(8,128)(2,1)S(1)} collective-permute-done((bf16[16,2048]{1,0:T(8,128)(2,1)S(1)}, bf16[16,2048]{1,0:T(8,128)(2,1)S(1)}, u32[]{:S(2)}, u32[]{:S(2)}) %collective-permute-start.1) | collective-permute-done | bytes 65568 | tf_op jit(solution)/shard_map/ppermute | solution.py:34
  12.1 2.0 %collective-permute-done.2.refs_3_ = bf16[16,2048]{1,0:T(8,128)(2,1)S(1)} collective-permute-done((bf16[16,2048]{1,0:T(8,128)(2,1)S(1)}, bf16[16,2048]{1,0:T(8,128)(2,1)S(1)}, u32[]{:S(2)}, u32[]{:S(2)}) %collective-permute-start.2) | collective-permute-done | bytes 65568 | tf_op jit(solution)/shard_map/ppermute | solution.py:34
  14.2 1.6 %collective-permute-start.3 = (bf16[4,16,2048]{2,1,0:T(8,128)(2,1)S(1)}, bf16[4,16,2048]{2,1,0:T(8,128)(2,1)S(1)}, u32[]{:S(2)}, u32[]{:S(2)}) collective-permute-start(bf16[4,16,2048]{2,1,0:T(8,128)(2,1)S(1)} %shard_map.85.refs_0_), channel_id=1, source_target_pairs={{0,2},{2,0},{4,6},{6,4},{8,10},{10,8},{12,14},{14,12},{1,3},{3,1},... | collective-permute-start | bytes 786440 | tf_op jit(solution)/shard_map/ppermute | solution.py:34
  15.7 1.4 %collective-permute-done.4 = bf16[16,7168]{1,0:T(8,128)(2,1)S(1)} collective-permute-done((bf16[16,7168]{1,0:T(8,128)(2,1)S(1)}, bf16[16,7168]{1,0:T(8,128)(2,1)S(1)}, u32[]{:S(2)}, u32[]{:S(2)}) %collective-permute-start.4) | collective-permute-done | bytes 229408 | tf_op jit(solution)/shard_map/ppermute | solution.py:34
  17.1 1.5 %collective-permute-start.10 = (bf16[16,7168]{1,0:T(8,128)(2,1)S(1)}, bf16[16,7168]{1,0:T(8,128)(2,1)S(1)}, u32[]{:S(2)}, u32[]{:S(2)}) collective-permute-start(bf16[16,7168]{1,0:T(8,128)(2,1)S(1)} %collective-permute-done.4), channel_id=1, source_target_pairs={{0,2},{2,0},{4,8},{6,10},{8,4},{10,6},{12,14},{14,12},{1,3},{3,1},... | collective-permute-start | bytes 688136 | tf_op jit(solution)/shard_map/ppermute | solution.py:88
  19.1 4.1 %collective-permute-done.3.refs_1_ = bf16[4,16,2048]{2,1,0:T(8,128)(2,1)S(1)} collective-permute-done((bf16[4,16,2048]{2,1,0:T(8,128)(2,1)S(1)}, bf16[4,16,2048]{2,1,0:T(8,128)(2,1)S(1)}, u32[]{:S(2)}, u32[]{:S(2)}) %collective-permute-start.3) | collective-permute-done | bytes 262176 | tf_op jit(solution)/shard_map/ppermute | solution.py:34
  23.3 0.7 %shard_map.86 = (f32[128,256]{1,0:T(8,128)S(1)}, f32[128,256]{1,0:T(8,128)S(1)}) custom-call(bf16[4,16,2048]{2,1,0:T(8,128)(2,1)S(1)} %shard_map.85.refs_0_, bf16[4,16,2048]{2,1,0:T(8,128)(2,1)S(1)} %collective-permute-done.3.refs_1_, bf16[2048,512]{1,0:T(8,128)(2,1)S(1)} %copy-done.1), custom_call_target="tpu_custom_call" | custom-call | flops 268435456 | bytes 2097152 | tf_op jit(solution)/shard_map/pallas_call | solution.py:21
  24.0 1.3 %collective-permute-done.6.b_ref = f32[128,256]{1,0:T(8,128)S(1)} collective-permute-done((f32[128,256]{1,0:T(8,128)S(1)}, f32[128,256]{1,0:T(8,128)S(1)}, u32[]{:S(2)}, u32[]{:S(2)}) %collective-permute-start.6) | collective-permute-done | bytes 131104 | tf_op jit(solution)/shard_map/ppermute | solution.py:34
  25.4 0.6 shard_map.87
  26.2 1.7 %collective-permute-start.13 = (bf16[16,7168]{1,0:T(8,128)(2,1)S(1)}, bf16[16,7168]{1,0:T(8,128)(2,1)S(1)}, u32[]{:S(2)}, u32[]{:S(2)}) collective-permute-start(bf16[16,7168]{1,0:T(8,128)(2,1)S(1)} %shard_map.88), channel_id=1, source_target_pairs={{0,2},{2,0},{4,6},{6,4},{8,10},{10,8},{12,14},{14,12},{1,3},{3,1},... | collective-permute-start | bytes 688136 | tf_op jit(solution)/shard_map/ppermute | solution.py:34
  27.9 2.0 %collective-permute-start.7 = (bf16[128,256]{1,0:T(8,128)(2,1)S(1)}, bf16[128,256]{1,0:T(8,128)(2,1)S(1)}, u32[]{:S(2)}, u32[]{:S(2)}) collective-permute-start(bf16[128,256]{1,0:T(8,128)(2,1)S(1)} %get-tuple-element.20.refs_0_), channel_id=1, source_target_pairs={{0,4},{2,6},{4,0},{6,2},{8,12},{10,14},{12,8},{14,10},{1,5},{3,7},... | collective-permute-start | bytes 196616 | tf_op jit(solution)/shard_map/ppermute | solution.py:34
  29.9 1.8 %collective-permute-start.8 = (bf16[128,256]{1,0:T(8,128)(2,1)S(1)}, bf16[128,256]{1,0:T(8,128)(2,1)S(1)}, u32[]{:S(2)}, u32[]{:S(2)}) collective-permute-start(bf16[128,256]{1,0:T(8,128)(2,1)S(1)} %get-tuple-element.20.refs_0_), channel_id=1, source_target_pairs={{0,8},{2,10},{4,12},{6,14},{8,0},{10,2},{12,4},{14,6},{1,9},{3,11}... | collective-permute-start | bytes 196616 | tf_op jit(solution)/shard_map/ppermute | solution.py:34
  31.6 1.5 %collective-permute-start.9 = (bf16[128,256]{1,0:T(8,128)(2,1)S(1)}, bf16[128,256]{1,0:T(8,128)(2,1)S(1)}, u32[]{:S(2)}, u32[]{:S(2)}) collective-permute-start(bf16[128,256]{1,0:T(8,128)(2,1)S(1)} %get-tuple-element.20.refs_0_), channel_id=1, source_target_pairs={{0,12},{2,14},{4,8},{6,10},{8,4},{10,6},{12,0},{14,2},{1,13},{3,15... | collective-permute-start | bytes 196616 | tf_op jit(solution)/shard_map/ppermute | solution.py:34
  33.1 3.4 %collective-permute-done.7.refs_1_ = bf16[128,256]{1,0:T(8,128)(2,1)S(1)} collective-permute-done((bf16[128,256]{1,0:T(8,128)(2,1)S(1)}, bf16[128,256]{1,0:T(8,128)(2,1)S(1)}, u32[]{:S(2)}, u32[]{:S(2)}) %collective-permute-start.7) | collective-permute-done | bytes 65568 | tf_op jit(solution)/shard_map/ppermute | solution.py:34
  36.5 3.1 %collective-permute-done.9.refs_3_ = bf16[128,256]{1,0:T(8,128)(2,1)S(1)} collective-permute-done((bf16[128,256]{1,0:T(8,128)(2,1)S(1)}, bf16[128,256]{1,0:T(8,128)(2,1)S(1)}, u32[]{:S(2)}, u32[]{:S(2)}) %collective-permute-start.9) | collective-permute-done | bytes 65568 | tf_op jit(solution)/shard_map/ppermute | solution.py:34
  39.7 1.5 %collective-permute-start.15 = (bf16[16,7168]{1,0:T(8,128)(2,1)S(1)}, bf16[16,7168]{1,0:T(8,128)(2,1)S(1)}, u32[]{:S(2)}, u32[]{:S(2)}) collective-permute-start(bf16[16,7168]{1,0:T(8,128)(2,1)S(1)} %shard_map.91), channel_id=1, source_target_pairs={{0,2},{2,0},{4,6},{6,4},{8,10},{10,8},{12,14},{14,12},{1,3},{3,1},... | collective-permute-start | bytes 688136 | tf_op jit(solution)/shard_map/ppermute | solution.py:34
  41.2 0.6 collective-permute-start.17
  41.9 1.3 %shard_map.90.refs_0_ = f32[2,128,896]{2,1,0:T(8,128)S(1)} custom-call(bf16[4,128,256]{2,1,0:T(8,128)(2,1)S(1)} %shard_map.89.mine, bf16[4,128,256]{2,1,0:T(8,128)(2,1)S(1)} %collective-permute-done.14.theirs, bf16[2,4096,896]{2,1,0:T(8,128)(2,1)S(1)} %bitcast.13), custom_call_target="tpu_custom_call" | custom-call | flops 939524096 | bytes 7340032 | tf_op jit(solution)/shard_map/pallas_call | solution.py:21
  43.1 5.1 %collective-permute-done.15 = bf16[16,7168]{1,0:T(8,128)(2,1)S(1)} collective-permute-done((bf16[16,7168]{1,0:T(8,128)(2,1)S(1)}, bf16[16,7168]{1,0:T(8,128)(2,1)S(1)}, u32[]{:S(2)}, u32[]{:S(2)}) %collective-permute-start.15) | collective-permute-done | bytes 229408 | tf_op jit(solution)/shard_map/ppermute | solution.py:34
  48.2 4.3 %shard_map.92 = (f32[128,896]{1,0:T(8,128)S(1)}, f32[128,896]{1,0:T(8,128)S(1)}) custom-call(bf16[1,16,7168]{2,1,0:T(8,128)(2,1)S(1)} %bitcast.15, bf16[1,16,7168]{2,1,0:T(8,128)(2,1)S(1)} %bitcast.20, bf16[1,16,7168]{2,1,0:T(8,128)(2,1)S(1)} %bitcast.16, bf16[1,16,7168]{2,1,0:T(8,128)(2,1)S(1)} %bitcast.17, bf16[1,16,7168]{2,1,0:T(8,128)(2,1)S(1)} %bitcast.18, ...), custom_call_target="tpu_custom_call" | custom-call | flops 11744051200 | bytes 25690112 | tf_op jit(solution)/shard_map/pallas_call | solution.py:21
  52.6 0.8 %collective-permute-done.17.mine = bf16[4,128,256]{2,1,0:T(8,128)(2,1)S(1)} collective-permute-done((bf16[4,128,256]{2,1,0:T(8,128)(2,1)S(1)}, bf16[4,128,256]{2,1,0:T(8,128)(2,1)S(1)}, u32[]{:S(2)}, u32[]{:S(2)}) %collective-permute-start.17) | collective-permute-done | bytes 262176 | tf_op jit(solution)/shard_map/ppermute | solution.py:34
  53.4 1.5 %collective-permute-done.18.theirs = bf16[4,128,256]{2,1,0:T(8,128)(2,1)S(1)} collective-permute-done((bf16[4,128,256]{2,1,0:T(8,128)(2,1)S(1)}, bf16[4,128,256]{2,1,0:T(8,128)(2,1)S(1)}, u32[]{:S(2)}, u32[]{:S(2)}) %collective-permute-start.18) | collective-permute-done | bytes 262176 | tf_op jit(solution)/shard_map/ppermute | solution.py:34
  54.9 1.3 %shard_map.93.wide = f32[2,128,896]{2,1,0:T(8,128)S(1)} custom-call(bf16[4,128,256]{2,1,0:T(8,128)(2,1)S(1)} %collective-permute-done.17.mine, bf16[4,128,256]{2,1,0:T(8,128)(2,1)S(1)} %collective-permute-done.18.theirs, bf16[2,4096,896]{2,1,0:T(8,128)(2,1)S(1)} %bitcast.13, f32[2,128,896]{2,1,0:T(8,128)S(1)} %shard_map.90.refs_0_), custom_call_target="tpu_custom_call" | custom-call | flops 939524096 | bytes 7340032 | tf_op jit(solution)/shard_map/pallas_call | solution.py:21
  56.2 0.8 %shard_map.94 = (bf16[128,896]{1,0:T(8,128)(2,1)}, f32[16,2,128]{2,1,0:T(2,128)S(1)}) custom-call(f32[128,896]{1,0:T(8,128)S(1)} %get-tuple-element.24.mine, f32[128,896]{1,0:T(8,128)S(1)} %collective-permute-done.16.theirs, f32[2,128,896]{2,1,0:T(8,128)S(1)} %shard_map.93.wide), custom_call_target="tpu_custom_call" | custom-call | tf_op jit(solution)/shard_map/pallas_call | solution.py:21
  57.0 10.3 %all_to_all.5 = f32[16,2,128]{2,1,0:T(2,128)S(1)} all-to-all(f32[16,2,128]{2,1,0:T(2,128)S(1)} %get-tuple-element.26), channel_id=1, replica_groups=mesh['parts'=2,'feat'=8,'tok'=2] {'feat','tok'}, dimensions={0} | all-to-all | bytes 32768 | tf_op jit(solution)/shard_map/all_to_all | solution.py:237
  67.3 0.6 reduce_sum.9
  (36 shorter events, 1.2 us)
Async XLA Ops:
  0.6 7.5 %copy-start = (bf16[16,7168]{1,0:T(8,128)(2,1)S(1)}, bf16[16,7168]{1,0:T(8,128)(2,1)}, u32[]{:S(2)}) copy-start(bf16[16,7168]{1,0:T(8,128)(2,1)} %param.7) | copy-start | bytes 688132
  1.7 6.4 %collective-permute-start = (bf16[16,2048]{1,0:T(8,128)(2,1)S(1)}, bf16[16,2048]{1,0:T(8,128)(2,1)S(1)}, u32[]{:S(2)}, u32[]{:S(2)}) collective-permute-start(bf16[16,2048]{1,0:T(8,128)(2,1)S(1)} %convolution_convert_fusion.1.refs_0_), channel_id=1, source_target_pairs={{0,4},{2,6},{4,0},{6,2},{8,12},{10,14},{12,8},{14,10},{1,5},{3,7},... | collective-permute-start | bytes 196616 | tf_op jit(solution)/shard_map/ppermute | solution.py:34
  4.8 7.3 %collective-permute-start.1 = (bf16[16,2048]{1,0:T(8,128)(2,1)S(1)}, bf16[16,2048]{1,0:T(8,128)(2,1)S(1)}, u32[]{:S(2)}, u32[]{:S(2)}) collective-permute-start(bf16[16,2048]{1,0:T(8,128)(2,1)S(1)} %convolution_convert_fusion.1.refs_0_), channel_id=1, source_target_pairs={{0,8},{2,10},{4,12},{6,14},{8,0},{10,2},{12,4},{14,6},{1,9},{3,11}... | collective-permute-start | bytes 196616 | tf_op jit(solution)/shard_map/ppermute | solution.py:34
  7.4 6.7 %collective-permute-start.2 = (bf16[16,2048]{1,0:T(8,128)(2,1)S(1)}, bf16[16,2048]{1,0:T(8,128)(2,1)S(1)}, u32[]{:S(2)}, u32[]{:S(2)}) collective-permute-start(bf16[16,2048]{1,0:T(8,128)(2,1)S(1)} %convolution_convert_fusion.1.refs_0_), channel_id=1, source_target_pairs={{0,12},{2,14},{4,8},{6,10},{8,4},{10,6},{12,0},{14,2},{1,13},{3,15... | collective-permute-start | bytes 196616 | tf_op jit(solution)/shard_map/ppermute | solution.py:34
  8.2 33.7 %slice-start = ((s8[14680064]{0:T(1024)(128)(4,1)}), s8[4194304]{0:T(1024)(128)(4,1)S(1)}, s32[]{:S(2)}) async-start(s8[14680064]{0:T(1024)(128)(4,1)} %bitcast.12), calls=%async_computation.1 | async-start | bytes 8388608
  8.4 14.9 %copy-start.1 = (bf16[2048,512]{1,0:T(8,128)(2,1)S(1)}, bf16[2048,512]{1,0:T(8,128)(2,1)}, u32[]{:S(2)}) copy-start(bf16[2048,512]{1,0:T(8,128)(2,1)} %refs_2_.1) | copy-start | bytes 6291460
  8.4 33.4 %slice-start.1 = ((s8[14680064]{0:T(1024)(128)(4,1)}), s8[4194304]{0:T(1024)(128)(4,1)S(1)}, s32[]{:S(2)}) async-start(s8[14680064]{0:T(1024)(128)(4,1)} %bitcast.12), calls=%async_computation.2 | async-start | bytes 8388608
  8.4 33.4 %slice-start.2 = ((s8[14680064]{0:T(1024)(128)(4,1)}), s8[4194304]{0:T(1024)(128)(4,1)S(1)}, s32[]{:S(2)}) async-start(s8[14680064]{0:T(1024)(128)(4,1)} %bitcast.12), calls=%async_computation.3 | async-start | bytes 8388608
  8.4 33.4 %slice-start.3 = ((s8[14680064]{0:T(1024)(128)(4,1)}), s8[2097152]{0:T(1024)(128)(4,1)S(1)}, s32[]{:S(2)}) async-start(s8[14680064]{0:T(1024)(128)(4,1)} %bitcast.12), calls=%async_computation.4 | async-start | bytes 4194304
  8.4 8.7 %collective-permute-start.4 = (bf16[16,7168]{1,0:T(8,128)(2,1)S(1)}, bf16[16,7168]{1,0:T(8,128)(2,1)S(1)}, u32[]{:S(2)}, u32[]{:S(2)}) collective-permute-start(bf16[16,7168]{1,0:T(8,128)(2,1)S(1)} %convolution_convert_fusion.refs_4_), channel_id=1, source_target_pairs={{0,4},{2,6},{4,0},{6,2},{8,12},{10,14},{12,8},{14,10},{1,5},{3,7},... | collective-permute-start | bytes 688136 | tf_op jit(solution)/shard_map/ppermute | solution.py:34
  9.4 9.2 %collective-permute-start.5 = (bf16[16,7168]{1,0:T(8,128)(2,1)S(1)}, bf16[16,7168]{1,0:T(8,128)(2,1)S(1)}, u32[]{:S(2)}, u32[]{:S(2)}) collective-permute-start(bf16[16,7168]{1,0:T(8,128)(2,1)S(1)} %convolution_convert_fusion.refs_4_), channel_id=1, source_target_pairs={{0,2},{2,0},{4,8},{6,10},{8,4},{10,6},{12,14},{14,12},{1,3},{3,1},... | collective-permute-start | bytes 688136 | tf_op jit(solution)/shard_map/ppermute | solution.py:88
  14.1 34.0 %copy-start.2 = (bf16[7168,1792]{1,0:T(8,128)(2,1)S(1)}, bf16[7168,1792]{1,0:T(8,128)(2,1)}, u32[]{:S(2)}) copy-start(bf16[7168,1792]{1,0:T(8,128)(2,1)} %refs_8_.1) | copy-start | bytes 77070336
  14.2 9.1 %collective-permute-start.3 = (bf16[4,16,2048]{2,1,0:T(8,128)(2,1)S(1)}, bf16[4,16,2048]{2,1,0:T(8,128)(2,1)S(1)}, u32[]{:S(2)}, u32[]{:S(2)}) collective-permute-start(bf16[4,16,2048]{2,1,0:T(8,128)(2,1)S(1)} %shard_map.85.refs_0_), channel_id=1, source_target_pairs={{0,2},{2,0},{4,6},{6,4},{8,10},{10,8},{12,14},{14,12},{1,3},{3,1},... | collective-permute-start | bytes 786440 | tf_op jit(solution)/shard_map/ppermute | solution.py:34
  17.1 9.0 %collective-permute-start.10 = (bf16[16,7168]{1,0:T(8,128)(2,1)S(1)}, bf16[16,7168]{1,0:T(8,128)(2,1)S(1)}, u32[]{:S(2)}, u32[]{:S(2)}) collective-permute-start(bf16[16,7168]{1,0:T(8,128)(2,1)S(1)} %collective-permute-done.4), channel_id=1, source_target_pairs={{0,2},{2,0},{4,8},{6,10},{8,4},{10,6},{12,14},{14,12},{1,3},{3,1},... | collective-permute-start | bytes 688136 | tf_op jit(solution)/shard_map/ppermute | solution.py:88
  18.6 7.5 %collective-permute-start.12 = (bf16[16,7168]{1,0:T(8,128)(2,1)S(1)}, bf16[16,7168]{1,0:T(8,128)(2,1)S(1)}, u32[]{:S(2)}, u32[]{:S(2)}) collective-permute-start(bf16[16,7168]{1,0:T(8,128)(2,1)S(1)} %collective-permute-done.5.inner_ref), channel_id=1, source_target_pairs={{0,4},{2,6},{4,0},{6,2},{8,12},{10,14},{12,8},{14,10},{1,5},{3,7},... | collective-permute-start | bytes 688136 | tf_op jit(solution)/shard_map/ppermute | solution.py:34
  24.0 1.4 %collective-permute-start.6 = (f32[128,256]{1,0:T(8,128)S(1)}, f32[128,256]{1,0:T(8,128)S(1)}, u32[]{:S(2)}, u32[]{:S(2)}) collective-permute-start(f32[128,256]{1,0:T(8,128)S(1)} %get-tuple-element.19), channel_id=1, source_target_pairs={{0,1},{1,0},{2,3},{3,2},{4,5},{5,4},{6,7},{7,6},{8,9},{9,8},{10,11... | collective-permute-start | bytes 393224 | tf_op jit(solution)/shard_map/ppermute | solution.py:34
  26.1 13.4 %collective-permute-start.11 = (bf16[16,7168]{1,0:T(8,128)(2,1)S(1)}, bf16[16,7168]{1,0:T(8,128)(2,1)S(1)}, u32[]{:S(2)}, u32[]{:S(2)}) collective-permute-start(bf16[16,7168]{1,0:T(8,128)(2,1)S(1)} %collective-permute-done.10.inner_ref), channel_id=1, source_target_pairs={{0,4},{2,6},{4,0},{6,2},{8,12},{10,14},{12,8},{14,10},{1,5},{3,7},... | collective-permute-start | bytes 688136 | tf_op jit(solution)/shard_map/ppermute | solution.py:34
  26.2 13.4 %collective-permute-start.13 = (bf16[16,7168]{1,0:T(8,128)(2,1)S(1)}, bf16[16,7168]{1,0:T(8,128)(2,1)S(1)}, u32[]{:S(2)}, u32[]{:S(2)}) collective-permute-start(bf16[16,7168]{1,0:T(8,128)(2,1)S(1)} %shard_map.88), channel_id=1, source_target_pairs={{0,2},{2,0},{4,6},{6,4},{8,10},{10,8},{12,14},{14,12},{1,3},{3,1},... | collective-permute-start | bytes 688136 | tf_op jit(solution)/shard_map/ppermute | solution.py:34
  27.9 8.6 %collective-permute-start.7 = (bf16[128,256]{1,0:T(8,128)(2,1)S(1)}, bf16[128,256]{1,0:T(8,128)(2,1)S(1)}, u32[]{:S(2)}, u32[]{:S(2)}) collective-permute-start(bf16[128,256]{1,0:T(8,128)(2,1)S(1)} %get-tuple-element.20.refs_0_), channel_id=1, source_target_pairs={{0,4},{2,6},{4,0},{6,2},{8,12},{10,14},{12,8},{14,10},{1,5},{3,7},... | collective-permute-start | bytes 196616 | tf_op jit(solution)/shard_map/ppermute | solution.py:34
  29.9 6.6 %collective-permute-start.8 = (bf16[128,256]{1,0:T(8,128)(2,1)S(1)}, bf16[128,256]{1,0:T(8,128)(2,1)S(1)}, u32[]{:S(2)}, u32[]{:S(2)}) collective-permute-start(bf16[128,256]{1,0:T(8,128)(2,1)S(1)} %get-tuple-element.20.refs_0_), channel_id=1, source_target_pairs={{0,8},{2,10},{4,12},{6,14},{8,0},{10,2},{12,4},{14,6},{1,9},{3,11}... | collective-permute-start | bytes 196616 | tf_op jit(solution)/shard_map/ppermute | solution.py:34
  31.6 7.9 %collective-permute-start.9 = (bf16[128,256]{1,0:T(8,128)(2,1)S(1)}, bf16[128,256]{1,0:T(8,128)(2,1)S(1)}, u32[]{:S(2)}, u32[]{:S(2)}) collective-permute-start(bf16[128,256]{1,0:T(8,128)(2,1)S(1)} %get-tuple-element.20.refs_0_), channel_id=1, source_target_pairs={{0,12},{2,14},{4,8},{6,10},{8,4},{10,6},{12,0},{14,2},{1,13},{3,15... | collective-permute-start | bytes 196616 | tf_op jit(solution)/shard_map/ppermute | solution.py:34
  39.6 2.2 %collective-permute-start.14 = (bf16[4,128,256]{2,1,0:T(8,128)(2,1)S(1)}, bf16[4,128,256]{2,1,0:T(8,128)(2,1)S(1)}, u32[]{:S(2)}, u32[]{:S(2)}) collective-permute-start(bf16[4,128,256]{2,1,0:T(8,128)(2,1)S(1)} %shard_map.89.mine), channel_id=1, source_target_pairs={{0,1},{1,0},{2,3},{3,2},{4,5},{5,4},{6,7},{7,6},{8,9},{9,8},{10,11... | collective-permute-start | bytes 786440 | tf_op jit(solution)/shard_map/ppermute | solution.py:34
  39.7 8.5 %collective-permute-start.15 = (bf16[16,7168]{1,0:T(8,128)(2,1)S(1)}, bf16[16,7168]{1,0:T(8,128)(2,1)S(1)}, u32[]{:S(2)}, u32[]{:S(2)}) collective-permute-start(bf16[16,7168]{1,0:T(8,128)(2,1)S(1)} %shard_map.91), channel_id=1, source_target_pairs={{0,2},{2,0},{4,6},{6,4},{8,10},{10,8},{12,14},{14,12},{1,3},{3,1},... | collective-permute-start | bytes 688136 | tf_op jit(solution)/shard_map/ppermute | solution.py:34
  41.2 12.2 %collective-permute-start.17 = (bf16[4,128,256]{2,1,0:T(8,128)(2,1)S(1)}, bf16[4,128,256]{2,1,0:T(8,128)(2,1)S(1)}, u32[]{:S(2)}, u32[]{:S(2)}) collective-permute-start(bf16[4,128,256]{2,1,0:T(8,128)(2,1)S(1)} %shard_map.89.mine), channel_id=1, source_target_pairs={{0,2},{2,0},{4,6},{6,4},{8,10},{10,8},{12,14},{14,12},{1,3},{3,1},... | collective-permute-start | bytes 786440 | tf_op jit(solution)/shard_map/ppermute | solution.py:34
  52.5 3.7 %collective-permute-start.16 = (f32[128,896]{1,0:T(8,128)S(1)}, f32[128,896]{1,0:T(8,128)S(1)}, u32[]{:S(2)}, u32[]{:S(2)}) collective-permute-start(f32[128,896]{1,0:T(8,128)S(1)} %get-tuple-element.25), channel_id=1, source_target_pairs={{0,1},{1,0},{2,3},{3,2},{4,5},{5,4},{6,7},{7,6},{8,9},{9,8},{10,11... | collective-permute-start | bytes 1376264 | tf_op jit(solution)/shard_map/ppermute | solution.py:34
  53.4 1.5 %collective-permute-start.18 = (bf16[4,128,256]{2,1,0:T(8,128)(2,1)S(1)}, bf16[4,128,256]{2,1,0:T(8,128)(2,1)S(1)}, u32[]{:S(2)}, u32[]{:S(2)}) collective-permute-start(bf16[4,128,256]{2,1,0:T(8,128)(2,1)S(1)} %collective-permute-done.17.mine), channel_id=1, source_target_pairs={{0,1},{1,0},{2,3},{3,2},{4,5},{5,4},{6,7},{7,6},{8,9},{9,8},{10,11... | collective-permute-start | bytes 786440 | tf_op jit(solution)/shard_map/ppermute | solution.py:34

commit v4 on v3

--- a/solution.py
+++ b/solution.py
@@ -148,39 +148,43 @@
     again[...] = total
 
 
-def query_kernel(side, mine, theirs, precond, *refs):
-    *so_far, out = refs
+def terms(side, flips, blocks, precond, q, total):
     me, tok = lax.axis_index("feat"), lax.axis_index("tok")
-    count, _, w = mine.shape
+    for flip, block in zip(flips, blocks):
+        count, _, w = block.shape
+        for j in range(count):
+            owner = ((me ^ (2 * j + side)) * 2 + (tok ^ flip)) * w
+            part = precond[q, pl.ds(pl.multiple_of(owner, w), w), :]
+            term = jnp.dot(block[j], part, preferred_element_type=F32)
+            total = term if total is None else total + term
+    return total
+
+
+def query_kernel(side, flips, *refs):
+    blocks, (precond, *so_far, out) = refs[:len(flips)], refs[len(flips):]
     for q in range(precond.shape[0]):
-        total = so_far[0][q] if so_far else None
-        for i, block in enumerate((mine, theirs)):
-            for j in range(count):
-                owner = ((me ^ (2 * j + side)) * 2 + (tok ^ i)) * w
-                part = precond[q, pl.ds(pl.multiple_of(owner, w), w), :]
-                term = jnp.dot(block[j], part, preferred_element_type=F32)
-                total = term if total is None else total + term
-        out[q] = total
-
-
-def query(side, mine, theirs, precond, so_far):
+        out[q] = terms(side, flips, blocks, precond, q, so_far[0][q] if so_far else None)
+
+
+def query(side, blocks, precond, so_far=()):
     queries, _, width = precond.shape
-    tokens = mine.shape[1]
+    tokens = next(iter(blocks.values())).shape[1]
     (out,) = call(
-        functools.partial(query_kernel, side), [((queries, tokens, width), F32)],
-        mine, theirs, precond, *so_far,
-        flops=tokens * precond.size, read=precond.size,
+        functools.partial(query_kernel, side, tuple(blocks)), [((queries, tokens, width), F32)],
+        *blocks.values(), precond, *so_far,
+        flops=len(blocks) * tokens * precond.size // 2, read=len(blocks) * precond.size // 2,
     )
     return out
 
 
-def score_kernel(mine, theirs, wide, act_rot, out):
+def score_kernel(mine, theirs, block, precond, wide, act_rot, out):
     rot = (mine[...] + theirs[...]).astype(BF16)
     act_rot[...] = rot
     rot = rot.astype(F32)
-    value = jnp.sum(wide[...] * rot[None], axis=2)
-    for i in range(out.shape[0]):
-        out[i] = value
+    for q in range(precond.shape[0]):
+        value = jnp.sum(terms(1, (1,), (block,), precond, q, wide[q]) * rot, axis=1)
+        for i in range(out.shape[0]):
+            out[i, q] = value
 
 
 def across(x):
@@ -224,15 +228,15 @@
         act_far = swap(bundle(act_near[1:], [block]), "feat", 1)
         mine = bundle(across(block))
         act_all, place = act_near + first + [act_far], direct
-    wide = query(0, mine, swap(mine, "tok", 1), precond, [])
+    wide = query(0, {0: mine, 1: swap(mine, "tok", 1)}, precond)
     other = swap(mine, "feat", 1)
     act_all[0] = after(act_all[0], wide)
-    wide = query(1, other, swap(other, "tok", 1), precond, [wide])
+    wide = query(1, {0: other}, precond, [wide])
     act_all = [x if x.ndim == 3 else x[None] for x in act_all]
     keep, give = rotate(act_all, place, basis_in, act_width // 4, 1600 * precond.size)
     act_rot, parts = call(
         score_kernel, [(keep.shape, BF16), ((2 * n, queries, tokens), F32)],
-        keep, swap(give, "tok", 1), wide,
+        keep, swap(give, "tok", 1), swap(other, "tok", 1), precond, wide,
     )
     scores = lax.all_to_all(parts, ("feat", "tok"), 0, 0, tiled=True).sum(axis=0)
     return scores, act_rot, grad_rot

time: 68.1 us -> 67.3 us (0.988)
  starting transfers between devices: 21 us -> 25.6 us
  waiting for transfers between devices: 24 us -> 19.4 us
  blocking collectives: 10.3 us -> 9.43 us
    ppermute x17, waiting for transfers between devices: 23.9 us -> 19 us  [swap(): return lax.ppermute(x, axis, [(i, i ^ step) for i in range(n)])]
    ppermute x17, starting transfers between devices: 18 us -> 22.3 us  [swap(): return lax.ppermute(x, axis, [(i, i ^ step) for i in range(n)])]
    all_to_all x1, blocking collectives: 10.3 us -> 9.43 us  [shards(): lax.all_to_all(parts, ('feat', 'tok'), 0, 0, tiled=True).sum(axis=0)]
  transfers between devices with their start and end apart: 19 -> 19, of which waited for: 11 -> 12; matrix products, arithmetic and copies ran while one was open for 1% -> 1% of each run, Pallas kernels for 12% -> 12%
where the time goes in v4:
time: 67.3 us; the launch traced here: 67.1 us
  starting transfers between devices  25.6 us (38%)
  waiting for transfers between devices  19.4 us (29%)
  blocking collectives  9.43 us (14%)
  Pallas kernels  9.22 us (14%)
  other arithmetic  1.31 us (2%)
  matrix products  1.29 us (2%)
  between operations  0.82 us (1%)
    ppermute x17, starting transfers between devices, swap(): return lax.ppermute(x, axis, [(i, i ^ step) for i in range(n)])  22.3 us
    ppermute x17, waiting for transfers between devices, swap(): return lax.ppermute(x, axis, [(i, i ^ step) for i in range(n)])  19 us
    all_to_all x1, blocking collectives, shards(): lax.all_to_all(parts, ('feat', 'tok'), 0, 0, tiled=True).sum(axis=0)  9.43 us
    pallas_call x10, Pallas kernels, call(): pl.pallas_call(kernel, in_specs=specs or [VMEM] * len(args), out_specs=[V...  9.22 us
    ppermute x2, starting transfers between devices, pair_middle(): return lax.ppermute(x, 'feat', list(enumerate(to)))  3.32 us
  transfers between devices with their start and end apart: 19, of which 12 were waited for; matrix products, arithmetic and copies ran while one was open for 1% of the time, Pallas kernels for 12%

profile of v4, /device:TPU:0, one launch (start us, length us, event | category | flops | bytes accessed | tf_op | source)
XLA Modules:
  0.0 67.1 jit_solution(1047546530532901601)
XLA Ops:
  0.6 1.1 %convolution_convert_fusion.1.refs_0_ = bf16[16,2048]{1,0:T(8,128)(2,1)S(1)} fusion(bf16[16,2048]{1,0:T(8,128)(2,1)} %param.8, s32[16]{0:T(128)} %bitcast.22), kind=kOutput, calls=%fused_computation.1 | convolution fusion | flops 1081600 | bytes 131136 | tf_op jit(solution)/shard_map/dot_general | solution.py:48
  1.7 3.1 %collective-permute-start = (bf16[16,2048]{1,0:T(8,128)(2,1)S(1)}, bf16[16,2048]{1,0:T(8,128)(2,1)S(1)}, u32[]{:S(2)}, u32[]{:S(2)}) collective-permute-start(bf16[16,2048]{1,0:T(8,128)(2,1)S(1)} %convolution_convert_fusion.1.refs_0_), channel_id=1, source_target_pairs={{0,4},{2,6},{4,0},{6,2},{8,12},{10,14},{12,8},{14,10},{1,5},{3,7},... | collective-permute-start | bytes 196616 | tf_op jit(solution)/shard_map/ppermute | solution.py:34
  4.8 2.6 %collective-permute-start.1 = (bf16[16,2048]{1,0:T(8,128)(2,1)S(1)}, bf16[16,2048]{1,0:T(8,128)(2,1)S(1)}, u32[]{:S(2)}, u32[]{:S(2)}) collective-permute-start(bf16[16,2048]{1,0:T(8,128)(2,1)S(1)} %convolution_convert_fusion.1.refs_0_), channel_id=1, source_target_pairs={{0,8},{2,10},{4,12},{6,14},{8,0},{10,2},{12,4},{14,6},{1,9},{3,11}... | collective-permute-start | bytes 196616 | tf_op jit(solution)/shard_map/ppermute | solution.py:34
  7.4 0.7 %fusion = bf16[16,16]{1,0:T(8,128)(2,1)S(1)} fusion(s32[16]{0:T(128)} %bitcast.23), kind=kLoop, calls=%fused_computation.3 | loop fusion | flops 512 | bytes 576 | tf_op jit(solution)/shard_map/convert_element_type | solution.py:45
  8.4 1.8 %collective-permute-start.5 = (bf16[16,7168]{1,0:T(8,128)(2,1)S(1)}, bf16[16,7168]{1,0:T(8,128)(2,1)S(1)}, u32[]{:S(2)}, u32[]{:S(2)}) collective-permute-start(bf16[16,7168]{1,0:T(8,128)(2,1)S(1)} %convolution_convert_fusion.refs_4_), channel_id=1, source_target_pairs={{0,2},{2,0},{4,8},{6,10},{8,4},{10,6},{12,14},{14,12},{1,3},{3,1},... | collective-permute-start | bytes 688136 | tf_op jit(solution)/shard_map/ppermute | solution.py:88
  10.2 1.0 %collective-permute-start.4 = (bf16[16,7168]{1,0:T(8,128)(2,1)S(1)}, bf16[16,7168]{1,0:T(8,128)(2,1)S(1)}, u32[]{:S(2)}, u32[]{:S(2)}) collective-permute-start(bf16[16,7168]{1,0:T(8,128)(2,1)S(1)} %convolution_convert_fusion.refs_4_), channel_id=1, source_target_pairs={{0,4},{2,6},{4,0},{6,2},{8,12},{10,14},{12,8},{14,10},{1,5},{3,7},... | collective-permute-start | bytes 688136 | tf_op jit(solution)/shard_map/ppermute | solution.py:34
  11.3 0.9 %collective-permute-done.1.refs_2_ = bf16[16,2048]{1,0:T(8,128)(2,1)S(1)} collective-permute-done((bf16[16,2048]{1,0:T(8,128)(2,1)S(1)}, bf16[16,2048]{1,0:T(8,128)(2,1)S(1)}, u32[]{:S(2)}, u32[]{:S(2)}) %collective-permute-start.1) | collective-permute-done | bytes 65568 | tf_op jit(solution)/shard_map/ppermute | solution.py:34
  12.2 1.5 %collective-permute-done.2.refs_3_ = bf16[16,2048]{1,0:T(8,128)(2,1)S(1)} collective-permute-done((bf16[16,2048]{1,0:T(8,128)(2,1)S(1)}, bf16[16,2048]{1,0:T(8,128)(2,1)S(1)}, u32[]{:S(2)}, u32[]{:S(2)}) %collective-permute-start.2) | collective-permute-done | bytes 65568 | tf_op jit(solution)/shard_map/ppermute | solution.py:34
  13.7 2.0 %collective-permute-start.3 = (bf16[4,16,2048]{2,1,0:T(8,128)(2,1)S(1)}, bf16[4,16,2048]{2,1,0:T(8,128)(2,1)S(1)}, u32[]{:S(2)}, u32[]{:S(2)}) collective-permute-start(bf16[4,16,2048]{2,1,0:T(8,128)(2,1)S(1)} %shard_map.85.refs_0_), channel_id=1, source_target_pairs={{0,2},{2,0},{4,6},{6,4},{8,10},{10,8},{12,14},{14,12},{1,3},{3,1},... | collective-permute-start | bytes 786440 | tf_op jit(solution)/shard_map/ppermute | solution.py:34
  16.1 2.9 %collective-permute-start.12 = (bf16[16,7168]{1,0:T(8,128)(2,1)S(1)}, bf16[16,7168]{1,0:T(8,128)(2,1)S(1)}, u32[]{:S(2)}, u32[]{:S(2)}) collective-permute-start(bf16[16,7168]{1,0:T(8,128)(2,1)S(1)} %collective-permute-done.5.inner_ref), channel_id=1, source_target_pairs={{0,4},{2,6},{4,0},{6,2},{8,12},{10,14},{12,8},{14,10},{1,5},{3,7},... | collective-permute-start | bytes 688136 | tf_op jit(solution)/shard_map/ppermute | solution.py:34
  19.0 1.5 %collective-permute-start.10 = (bf16[16,7168]{1,0:T(8,128)(2,1)S(1)}, bf16[16,7168]{1,0:T(8,128)(2,1)S(1)}, u32[]{:S(2)}, u32[]{:S(2)}) collective-permute-start(bf16[16,7168]{1,0:T(8,128)(2,1)S(1)} %collective-permute-done.4), channel_id=1, source_target_pairs={{0,2},{2,0},{4,8},{6,10},{8,4},{10,6},{12,14},{14,12},{1,3},{3,1},... | collective-permute-start | bytes 688136 | tf_op jit(solution)/shard_map/ppermute | solution.py:88
  20.5 0.6 collective-permute-done.3.refs_1_
  21.1 0.7 %shard_map.86 = (f32[128,256]{1,0:T(8,128)S(1)}, f32[128,256]{1,0:T(8,128)S(1)}) custom-call(bf16[4,16,2048]{2,1,0:T(8,128)(2,1)S(1)} %shard_map.85.refs_0_, bf16[4,16,2048]{2,1,0:T(8,128)(2,1)S(1)} %collective-permute-done.3.refs_1_, bf16[2048,512]{1,0:T(8,128)(2,1)S(1)} %copy-done.1), custom_call_target="tpu_custom_call" | custom-call | flops 268435456 | bytes 2097152 | tf_op jit(solution)/shard_map/pallas_call | solution.py:21
  21.9 1.3 %collective-permute-done.6.b_ref = f32[128,256]{1,0:T(8,128)S(1)} collective-permute-done((f32[128,256]{1,0:T(8,128)S(1)}, f32[128,256]{1,0:T(8,128)S(1)}, u32[]{:S(2)}, u32[]{:S(2)}) %collective-permute-start.6) | collective-permute-done | bytes 131104 | tf_op jit(solution)/shard_map/ppermute | solution.py:34
  23.2 0.6 shard_map.87
  24.1 1.6 %collective-permute-start.13 = (bf16[16,7168]{1,0:T(8,128)(2,1)S(1)}, bf16[16,7168]{1,0:T(8,128)(2,1)S(1)}, u32[]{:S(2)}, u32[]{:S(2)}) collective-permute-start(bf16[16,7168]{1,0:T(8,128)(2,1)S(1)} %shard_map.88), channel_id=1, source_target_pairs={{0,2},{2,0},{4,6},{6,4},{8,10},{10,8},{12,14},{14,12},{1,3},{3,1},... | collective-permute-start | bytes 688136 | tf_op jit(solution)/shard_map/ppermute | solution.py:34
  25.8 1.6 %collective-permute-start.11 = (bf16[16,7168]{1,0:T(8,128)(2,1)S(1)}, bf16[16,7168]{1,0:T(8,128)(2,1)S(1)}, u32[]{:S(2)}, u32[]{:S(2)}) collective-permute-start(bf16[16,7168]{1,0:T(8,128)(2,1)S(1)} %collective-permute-done.10.inner_ref), channel_id=1, source_target_pairs={{0,4},{2,6},{4,0},{6,2},{8,12},{10,14},{12,8},{14,10},{1,5},{3,7},... | collective-permute-start | bytes 688136 | tf_op jit(solution)/shard_map/ppermute | solution.py:34
  27.8 3.3 %collective-permute-start.8 = (bf16[128,256]{1,0:T(8,128)(2,1)S(1)}, bf16[128,256]{1,0:T(8,128)(2,1)S(1)}, u32[]{:S(2)}, u32[]{:S(2)}) collective-permute-start(bf16[128,256]{1,0:T(8,128)(2,1)S(1)} %get-tuple-element.20.refs_0_), channel_id=1, source_target_pairs={{0,8},{2,10},{4,12},{6,14},{8,0},{10,2},{12,4},{14,6},{1,9},{3,11}... | collective-permute-start | bytes 196616 | tf_op jit(solution)/shard_map/ppermute | solution.py:34
  31.1 1.4 %collective-permute-start.9 = (bf16[128,256]{1,0:T(8,128)(2,1)S(1)}, bf16[128,256]{1,0:T(8,128)(2,1)S(1)}, u32[]{:S(2)}, u32[]{:S(2)}) collective-permute-start(bf16[128,256]{1,0:T(8,128)(2,1)S(1)} %get-tuple-element.20.refs_0_), channel_id=1, source_target_pairs={{0,12},{2,14},{4,8},{6,10},{8,4},{10,6},{12,0},{14,2},{1,13},{3,15... | collective-permute-start | bytes 196616 | tf_op jit(solution)/shard_map/ppermute | solution.py:34
  32.5 3.2 %collective-permute-done.7.refs_1_ = bf16[128,256]{1,0:T(8,128)(2,1)S(1)} collective-permute-done((bf16[128,256]{1,0:T(8,128)(2,1)S(1)}, bf16[128,256]{1,0:T(8,128)(2,1)S(1)}, u32[]{:S(2)}, u32[]{:S(2)}) %collective-permute-start.7) | collective-permute-done | bytes 65568 | tf_op jit(solution)/shard_map/ppermute | solution.py:34
  35.7 4.6 %collective-permute-done.9.refs_3_ = bf16[128,256]{1,0:T(8,128)(2,1)S(1)} collective-permute-done((bf16[128,256]{1,0:T(8,128)(2,1)S(1)}, bf16[128,256]{1,0:T(8,128)(2,1)S(1)}, u32[]{:S(2)}, u32[]{:S(2)}) %collective-permute-start.9) | collective-permute-done | bytes 65568 | tf_op jit(solution)/shard_map/ppermute | solution.py:34
  40.5 0.6 collective-permute-start.15
  41.1 1.5 %collective-permute-start.17 = (bf16[4,128,256]{2,1,0:T(8,128)(2,1)S(1)}, bf16[4,128,256]{2,1,0:T(8,128)(2,1)S(1)}, u32[]{:S(2)}, u32[]{:S(2)}) collective-permute-start(bf16[4,128,256]{2,1,0:T(8,128)(2,1)S(1)} %shard_map.89.refs_0_), channel_id=1, source_target_pairs={{0,2},{2,0},{4,6},{6,4},{8,10},{10,8},{12,14},{14,12},{1,3},{3,1},... | collective-permute-start | bytes 786440 | tf_op jit(solution)/shard_map/ppermute | solution.py:34
  42.6 1.3 %shard_map.90.refs_2_ = f32[2,128,896]{2,1,0:T(8,128)S(1)} custom-call(bf16[4,128,256]{2,1,0:T(8,128)(2,1)S(1)} %shard_map.89.refs_0_, bf16[4,128,256]{2,1,0:T(8,128)(2,1)S(1)} %collective-permute-done.14.refs_1_, bf16[2,4096,896]{2,1,0:T(8,128)(2,1)S(1)} %bitcast.13), custom_call_target="tpu_custom_call" | custom-call | flops 939524096 | bytes 7340032 | tf_op jit(solution)/shard_map/pallas_call | solution.py:21
  43.9 5.1 %collective-permute-done.15 = bf16[16,7168]{1,0:T(8,128)(2,1)S(1)} collective-permute-done((bf16[16,7168]{1,0:T(8,128)(2,1)S(1)}, bf16[16,7168]{1,0:T(8,128)(2,1)S(1)}, u32[]{:S(2)}, u32[]{:S(2)}) %collective-permute-start.15) | collective-permute-done | bytes 229408 | tf_op jit(solution)/shard_map/ppermute | solution.py:34
  49.0 4.3 %shard_map.92 = (f32[128,896]{1,0:T(8,128)S(1)}, f32[128,896]{1,0:T(8,128)S(1)}) custom-call(bf16[1,16,7168]{2,1,0:T(8,128)(2,1)S(1)} %bitcast.15, bf16[1,16,7168]{2,1,0:T(8,128)(2,1)S(1)} %bitcast.20, bf16[1,16,7168]{2,1,0:T(8,128)(2,1)S(1)} %bitcast.16, bf16[1,16,7168]{2,1,0:T(8,128)(2,1)S(1)} %bitcast.18, bf16[1,16,7168]{2,1,0:T(8,128)(2,1)S(1)} %bitcast.17, ...), custom_call_target="tpu_custom_call" | custom-call | flops 11744051200 | bytes 25690112 | tf_op jit(solution)/shard_map/pallas_call | solution.py:21
  53.4 0.8 %collective-permute-done.17.refs_0_ = bf16[4,128,256]{2,1,0:T(8,128)(2,1)S(1)} collective-permute-done((bf16[4,128,256]{2,1,0:T(8,128)(2,1)S(1)}, bf16[4,128,256]{2,1,0:T(8,128)(2,1)S(1)}, u32[]{:S(2)}, u32[]{:S(2)}) %collective-permute-start.17) | collective-permute-done | bytes 262176 | tf_op jit(solution)/shard_map/ppermute | solution.py:34
  54.2 0.7 %shard_map.93.wide = f32[2,128,896]{2,1,0:T(8,128)S(1)} custom-call(bf16[4,128,256]{2,1,0:T(8,128)(2,1)S(1)} %collective-permute-done.17.refs_0_, bf16[2,4096,896]{2,1,0:T(8,128)(2,1)S(1)} %bitcast.13, f32[2,128,896]{2,1,0:T(8,128)S(1)} %shard_map.90.refs_2_), custom_call_target="tpu_custom_call" | custom-call | flops 469762048 | bytes 3670016 | tf_op jit(solution)/shard_map/pallas_call | solution.py:21
  54.9 0.8 %collective-permute-done.18.block = bf16[4,128,256]{2,1,0:T(8,128)(2,1)S(1)} collective-permute-done((bf16[4,128,256]{2,1,0:T(8,128)(2,1)S(1)}, bf16[4,128,256]{2,1,0:T(8,128)(2,1)S(1)}, u32[]{:S(2)}, u32[]{:S(2)}) %collective-permute-start.18) | collective-permute-done | bytes 262176 | tf_op jit(solution)/shard_map/ppermute | solution.py:34
  55.7 1.4 %shard_map.94 = (bf16[128,896]{1,0:T(8,128)(2,1)}, f32[16,2,128]{2,1,0:T(2,128)S(1)}) custom-call(f32[128,896]{1,0:T(8,128)S(1)} %get-tuple-element.24.mine, f32[128,896]{1,0:T(8,128)S(1)} %collective-permute-done.16.theirs, bf16[4,128,256]{2,1,0:T(8,128)(2,1)S(1)} %collective-permute-done.18.block, bf16[2,4096,896]{2,1,0:T(8,128)(2,1)S(1)} %bitcast.13, ...), custom_call_target="tpu_custom_call" | custom-call | tf_op jit(solution)/shard_map/pallas_call | solution.py:21
  57.1 9.4 %all_to_all.5 = f32[16,2,128]{2,1,0:T(2,128)S(1)} all-to-all(f32[16,2,128]{2,1,0:T(2,128)S(1)} %get-tuple-element.26), channel_id=1, replica_groups=mesh['parts'=2,'feat'=8,'tok'=2] {'feat','tok'}, dimensions={0} | all-to-all | bytes 32768 | tf_op jit(solution)/shard_map/all_to_all | solution.py:241
  66.6 0.6 reduce_sum.9
  (36 shorter events, 1.6 us)
Async XLA Ops:
  0.6 7.5 %copy-start = (bf16[16,7168]{1,0:T(8,128)(2,1)S(1)}, bf16[16,7168]{1,0:T(8,128)(2,1)}, u32[]{:S(2)}) copy-start(bf16[16,7168]{1,0:T(8,128)(2,1)} %param.7) | copy-start | bytes 688132
  1.7 6.4 %collective-permute-start = (bf16[16,2048]{1,0:T(8,128)(2,1)S(1)}, bf16[16,2048]{1,0:T(8,128)(2,1)S(1)}, u32[]{:S(2)}, u32[]{:S(2)}) collective-permute-start(bf16[16,2048]{1,0:T(8,128)(2,1)S(1)} %convolution_convert_fusion.1.refs_0_), channel_id=1, source_target_pairs={{0,4},{2,6},{4,0},{6,2},{8,12},{10,14},{12,8},{14,10},{1,5},{3,7},... | collective-permute-start | bytes 196616 | tf_op jit(solution)/shard_map/ppermute | solution.py:34
  4.8 7.4 %collective-permute-start.1 = (bf16[16,2048]{1,0:T(8,128)(2,1)S(1)}, bf16[16,2048]{1,0:T(8,128)(2,1)S(1)}, u32[]{:S(2)}, u32[]{:S(2)}) collective-permute-start(bf16[16,2048]{1,0:T(8,128)(2,1)S(1)} %convolution_convert_fusion.1.refs_0_), channel_id=1, source_target_pairs={{0,8},{2,10},{4,12},{6,14},{8,0},{10,2},{12,4},{14,6},{1,9},{3,11}... | collective-permute-start | bytes 196616 | tf_op jit(solution)/shard_map/ppermute | solution.py:34
  7.4 6.2 %collective-permute-start.2 = (bf16[16,2048]{1,0:T(8,128)(2,1)S(1)}, bf16[16,2048]{1,0:T(8,128)(2,1)S(1)}, u32[]{:S(2)}, u32[]{:S(2)}) collective-permute-start(bf16[16,2048]{1,0:T(8,128)(2,1)S(1)} %convolution_convert_fusion.1.refs_0_), channel_id=1, source_target_pairs={{0,12},{2,14},{4,8},{6,10},{8,4},{10,6},{12,0},{14,2},{1,13},{3,15... | collective-permute-start | bytes 196616 | tf_op jit(solution)/shard_map/ppermute | solution.py:34
  8.2 34.4 %slice-start = ((s8[14680064]{0:T(1024)(128)(4,1)}), s8[4194304]{0:T(1024)(128)(4,1)S(1)}, s32[]{:S(2)}) async-start(s8[14680064]{0:T(1024)(128)(4,1)} %bitcast.12), calls=%async_computation.1 | async-start | bytes 8388608
  8.4 12.7 %copy-start.1 = (bf16[2048,512]{1,0:T(8,128)(2,1)S(1)}, bf16[2048,512]{1,0:T(8,128)(2,1)}, u32[]{:S(2)}) copy-start(bf16[2048,512]{1,0:T(8,128)(2,1)} %refs_2_.2) | copy-start | bytes 6291460
  8.4 34.2 %slice-start.1 = ((s8[14680064]{0:T(1024)(128)(4,1)}), s8[4194304]{0:T(1024)(128)(4,1)S(1)}, s32[]{:S(2)}) async-start(s8[14680064]{0:T(1024)(128)(4,1)} %bitcast.12), calls=%async_computation.2 | async-start | bytes 8388608
  8.4 34.2 %slice-start.2 = ((s8[14680064]{0:T(1024)(128)(4,1)}), s8[4194304]{0:T(1024)(128)(4,1)S(1)}, s32[]{:S(2)}) async-start(s8[14680064]{0:T(1024)(128)(4,1)} %bitcast.12), calls=%async_computation.3 | async-start | bytes 8388608
  8.4 34.2 %slice-start.3 = ((s8[14680064]{0:T(1024)(128)(4,1)}), s8[2097152]{0:T(1024)(128)(4,1)S(1)}, s32[]{:S(2)}) async-start(s8[14680064]{0:T(1024)(128)(4,1)} %bitcast.12), calls=%async_computation.4 | async-start | bytes 4194304
  8.4 7.6 %collective-permute-start.5 = (bf16[16,7168]{1,0:T(8,128)(2,1)S(1)}, bf16[16,7168]{1,0:T(8,128)(2,1)S(1)}, u32[]{:S(2)}, u32[]{:S(2)}) collective-permute-start(bf16[16,7168]{1,0:T(8,128)(2,1)S(1)} %convolution_convert_fusion.refs_4_), channel_id=1, source_target_pairs={{0,2},{2,0},{4,8},{6,10},{8,4},{10,6},{12,14},{14,12},{1,3},{3,1},... | collective-permute-start | bytes 688136 | tf_op jit(solution)/shard_map/ppermute | solution.py:88
  10.2 8.8 %collective-permute-start.4 = (bf16[16,7168]{1,0:T(8,128)(2,1)S(1)}, bf16[16,7168]{1,0:T(8,128)(2,1)S(1)}, u32[]{:S(2)}, u32[]{:S(2)}) collective-permute-start(bf16[16,7168]{1,0:T(8,128)(2,1)S(1)} %convolution_convert_fusion.refs_4_), channel_id=1, source_target_pairs={{0,4},{2,6},{4,0},{6,2},{8,12},{10,14},{12,8},{14,10},{1,5},{3,7},... | collective-permute-start | bytes 688136 | tf_op jit(solution)/shard_map/ppermute | solution.py:34
  13.7 35.3 %copy-start.2 = (bf16[7168,1792]{1,0:T(8,128)(2,1)S(1)}, bf16[7168,1792]{1,0:T(8,128)(2,1)}, u32[]{:S(2)}) copy-start(bf16[7168,1792]{1,0:T(8,128)(2,1)} %refs_8_.1) | copy-start | bytes 77070336
  13.7 7.4 %collective-permute-start.3 = (bf16[4,16,2048]{2,1,0:T(8,128)(2,1)S(1)}, bf16[4,16,2048]{2,1,0:T(8,128)(2,1)S(1)}, u32[]{:S(2)}, u32[]{:S(2)}) collective-permute-start(bf16[4,16,2048]{2,1,0:T(8,128)(2,1)S(1)} %shard_map.85.refs_0_), channel_id=1, source_target_pairs={{0,2},{2,0},{4,6},{6,4},{8,10},{10,8},{12,14},{14,12},{1,3},{3,1},... | collective-permute-start | bytes 786440 | tf_op jit(solution)/shard_map/ppermute | solution.py:34
  16.1 8.0 %collective-permute-start.12 = (bf16[16,7168]{1,0:T(8,128)(2,1)S(1)}, bf16[16,7168]{1,0:T(8,128)(2,1)S(1)}, u32[]{:S(2)}, u32[]{:S(2)}) collective-permute-start(bf16[16,7168]{1,0:T(8,128)(2,1)S(1)} %collective-permute-done.5.inner_ref), channel_id=1, source_target_pairs={{0,4},{2,6},{4,0},{6,2},{8,12},{10,14},{12,8},{14,10},{1,5},{3,7},... | collective-permute-start | bytes 688136 | tf_op jit(solution)/shard_map/ppermute | solution.py:34
  19.0 6.8 %collective-permute-start.10 = (bf16[16,7168]{1,0:T(8,128)(2,1)S(1)}, bf16[16,7168]{1,0:T(8,128)(2,1)S(1)}, u32[]{:S(2)}, u32[]{:S(2)}) collective-permute-start(bf16[16,7168]{1,0:T(8,128)(2,1)S(1)} %collective-permute-done.4), channel_id=1, source_target_pairs={{0,2},{2,0},{4,8},{6,10},{8,4},{10,6},{12,14},{14,12},{1,3},{3,1},... | collective-permute-start | bytes 688136 | tf_op jit(solution)/shard_map/ppermute | solution.py:88
  21.8 1.4 %collective-permute-start.6 = (f32[128,256]{1,0:T(8,128)S(1)}, f32[128,256]{1,0:T(8,128)S(1)}, u32[]{:S(2)}, u32[]{:S(2)}) collective-permute-start(f32[128,256]{1,0:T(8,128)S(1)} %get-tuple-element.19), channel_id=1, source_target_pairs={{0,1},{1,0},{2,3},{3,2},{4,5},{5,4},{6,7},{7,6},{8,9},{9,8},{10,11... | collective-permute-start | bytes 393224 | tf_op jit(solution)/shard_map/ppermute | solution.py:34
  24.1 16.2 %collective-permute-start.13 = (bf16[16,7168]{1,0:T(8,128)(2,1)S(1)}, bf16[16,7168]{1,0:T(8,128)(2,1)S(1)}, u32[]{:S(2)}, u32[]{:S(2)}) collective-permute-start(bf16[16,7168]{1,0:T(8,128)(2,1)S(1)} %shard_map.88), channel_id=1, source_target_pairs={{0,2},{2,0},{4,6},{6,4},{8,10},{10,8},{12,14},{14,12},{1,3},{3,1},... | collective-permute-start | bytes 688136 | tf_op jit(solution)/shard_map/ppermute | solution.py:34
  25.8 14.5 %collective-permute-start.11 = (bf16[16,7168]{1,0:T(8,128)(2,1)S(1)}, bf16[16,7168]{1,0:T(8,128)(2,1)S(1)}, u32[]{:S(2)}, u32[]{:S(2)}) collective-permute-start(bf16[16,7168]{1,0:T(8,128)(2,1)S(1)} %collective-permute-done.10.inner_ref), channel_id=1, source_target_pairs={{0,4},{2,6},{4,0},{6,2},{8,12},{10,14},{12,8},{14,10},{1,5},{3,7},... | collective-permute-start | bytes 688136 | tf_op jit(solution)/shard_map/ppermute | solution.py:34
  27.4 8.3 %collective-permute-start.7 = (bf16[128,256]{1,0:T(8,128)(2,1)S(1)}, bf16[128,256]{1,0:T(8,128)(2,1)S(1)}, u32[]{:S(2)}, u32[]{:S(2)}) collective-permute-start(bf16[128,256]{1,0:T(8,128)(2,1)S(1)} %get-tuple-element.20.refs_0_), channel_id=1, source_target_pairs={{0,4},{2,6},{4,0},{6,2},{8,12},{10,14},{12,8},{14,10},{1,5},{3,7},... | collective-permute-start | bytes 196616 | tf_op jit(solution)/shard_map/ppermute | solution.py:34
  27.8 7.9 %collective-permute-start.8 = (bf16[128,256]{1,0:T(8,128)(2,1)S(1)}, bf16[128,256]{1,0:T(8,128)(2,1)S(1)}, u32[]{:S(2)}, u32[]{:S(2)}) collective-permute-start(bf16[128,256]{1,0:T(8,128)(2,1)S(1)} %get-tuple-element.20.refs_0_), channel_id=1, source_target_pairs={{0,8},{2,10},{4,12},{6,14},{8,0},{10,2},{12,4},{14,6},{1,9},{3,11}... | collective-permute-start | bytes 196616 | tf_op jit(solution)/shard_map/ppermute | solution.py:34
  31.1 9.2 %collective-permute-start.9 = (bf16[128,256]{1,0:T(8,128)(2,1)S(1)}, bf16[128,256]{1,0:T(8,128)(2,1)S(1)}, u32[]{:S(2)}, u32[]{:S(2)}) collective-permute-start(bf16[128,256]{1,0:T(8,128)(2,1)S(1)} %get-tuple-element.20.refs_0_), channel_id=1, source_target_pairs={{0,12},{2,14},{4,8},{6,10},{8,4},{10,6},{12,0},{14,2},{1,13},{3,15... | collective-permute-start | bytes 196616 | tf_op jit(solution)/shard_map/ppermute | solution.py:34
  40.4 2.2 %collective-permute-start.14 = (bf16[4,128,256]{2,1,0:T(8,128)(2,1)S(1)}, bf16[4,128,256]{2,1,0:T(8,128)(2,1)S(1)}, u32[]{:S(2)}, u32[]{:S(2)}) collective-permute-start(bf16[4,128,256]{2,1,0:T(8,128)(2,1)S(1)} %shard_map.89.refs_0_), channel_id=1, source_target_pairs={{0,1},{1,0},{2,3},{3,2},{4,5},{5,4},{6,7},{7,6},{8,9},{9,8},{10,11... | collective-permute-start | bytes 786440 | tf_op jit(solution)/shard_map/ppermute | solution.py:34
  40.5 8.5 %collective-permute-start.15 = (bf16[16,7168]{1,0:T(8,128)(2,1)S(1)}, bf16[16,7168]{1,0:T(8,128)(2,1)S(1)}, u32[]{:S(2)}, u32[]{:S(2)}) collective-permute-start(bf16[16,7168]{1,0:T(8,128)(2,1)S(1)} %shard_map.91), channel_id=1, source_target_pairs={{0,2},{2,0},{4,6},{6,4},{8,10},{10,8},{12,14},{14,12},{1,3},{3,1},... | collective-permute-start | bytes 688136 | tf_op jit(solution)/shard_map/ppermute | solution.py:34
  41.1 13.1 %collective-permute-start.17 = (bf16[4,128,256]{2,1,0:T(8,128)(2,1)S(1)}, bf16[4,128,256]{2,1,0:T(8,128)(2,1)S(1)}, u32[]{:S(2)}, u32[]{:S(2)}) collective-permute-start(bf16[4,128,256]{2,1,0:T(8,128)(2,1)S(1)} %shard_map.89.refs_0_), channel_id=1, source_target_pairs={{0,2},{2,0},{4,6},{6,4},{8,10},{10,8},{12,14},{14,12},{1,3},{3,1},... | collective-permute-start | bytes 786440 | tf_op jit(solution)/shard_map/ppermute | solution.py:34
  53.3 2.4 %collective-permute-start.16 = (f32[128,896]{1,0:T(8,128)S(1)}, f32[128,896]{1,0:T(8,128)S(1)}, u32[]{:S(2)}, u32[]{:S(2)}) collective-permute-start(f32[128,896]{1,0:T(8,128)S(1)} %get-tuple-element.25), channel_id=1, source_target_pairs={{0,1},{1,0},{2,3},{3,2},{4,5},{5,4},{6,7},{7,6},{8,9},{9,8},{10,11... | collective-permute-start | bytes 1376264 | tf_op jit(solution)/shard_map/ppermute | solution.py:34
  54.2 1.5 %collective-permute-start.18 = (bf16[4,128,256]{2,1,0:T(8,128)(2,1)S(1)}, bf16[4,128,256]{2,1,0:T(8,128)(2,1)S(1)}, u32[]{:S(2)}, u32[]{:S(2)}) collective-permute-start(bf16[4,128,256]{2,1,0:T(8,128)(2,1)S(1)} %collective-permute-done.17.refs_0_), channel_id=1, source_target_pairs={{0,1},{1,0},{2,3},{3,2},{4,5},{5,4},{6,7},{7,6},{8,9},{9,8},{10,11... | collective-permute-start | bytes 786440 | tf_op jit(solution)/shard_map/ppermute | solution.py:34
